TPU v7x, 32 devices: a whole 2x2x4 slice. The times are simulated.
32 devices in a mesh: groups: 2 (over x), tensor: 4 (over y, core), dp: 4 (over z).
Axes of the slice: x: 2, y: 2, z: 4, core: 2. Of those that a mesh axis runs over, the one named last changes fastest.
Arguments:
- layer_input: bfloat16 [1024, 8192], P(('groups', 'dp'), 'tensor'), parts along dimension 0, may hold values from -6 to 6
- out_grad: bfloat16 [1024, 8192], P(('groups', 'dp'), 'tensor'), parts along dimension 0, may hold values from -6 to 6
- gate_pre: bfloat16 [1024, 14336], P(('groups', 'tensor'), 'dp'), parts along dimension 0, may hold values from -6 to 6
- up_pre: bfloat16 [1024, 14336], P(('groups', 'tensor'), 'dp'), parts along dimension 0, may hold values from -6 to 6
- adapter_acts: bfloat16 [1024, 48], P('groups'), parts along dimension 0, may hold values from -6 to 6
- gate_weight: bfloat16 [8192, 14336], P('tensor', 'dp'), may hold values from -0.0625 to 0.0625
- up_weight: bfloat16 [8192, 14336], P('tensor', 'dp'), may hold values from -0.0625 to 0.0625
- down_weight: bfloat16 [14336, 8192], P('dp', 'tensor'), may hold values from -0.046875 to 0.046875
- adapter_a_gu: bfloat16 [4, 8192, 32], P(None, 'tensor'), may hold values from -0.5 to 0.5
- adapter_b_gu: bfloat16 [4, 32, 14336], P(None, None, 'dp'), may hold values from -0.046875 to 0.046875
- adapter_a_down: bfloat16 [4, 14336, 16], P(None, 'dp'), may hold values from -0.75 to 0.75
- adapter_b_down: bfloat16 [4, 16, 8192], P(None, None, 'tensor'), may hold values from -0.0625 to 0.0625
- block_tenant: int32 [8], P('groups'), parts along dimension 0, may hold values from 0 to 3, as said below
Outputs:
- block_input_grad: bfloat16 [1024, 8192], P(('groups', 'dp'), 'tensor'), parts along dimension 0
- grad_a_gu: float32 [8, 8192, 32], P('groups', 'tensor'), parts along dimension 0
- grad_b_gu: float32 [8, 32, 14336], P('groups', None, 'dp'), parts along dimension 0
- grad_a_down: float32 [8, 14336, 16], P('groups', 'dp'), parts along dimension 0
- grad_b_down: float32 [8, 16, 8192], P('groups', None, 'tensor'), parts along dimension 0
There are 2 independent parts, one for each index of `groups`. A program takes and returns all parts, laid end to end along the dimension named above; an argument that names none is the same for every part. Nothing has to cross between parts.
Inputs may be any that keep to these rules, and one draw needn't show every extreme that they name: `block_tenant`: entry b names the tenant of tokens b * 128 to (b + 1) * 128 - 1. Every tenant owns at least one block, and the block counts of any two tenants differ by at most one.
All inputs are finite; a program needn't handle non-finite values.
Results may differ from a plain program's by a relative error of at most 0.017.
Values may be sent and summed in bfloat16 or wider, within the bound.
No kernel may reach another device: no remote copies, remote signals or barrier semaphores. Data moves between devices by JAX's collectives and lax.ppermute only.
A program may use at most 192 MiB of HBM per device.

v0:
```python
import functools

import jax
import jax.numpy as jnp
from jax import lax
from jax.experimental import pallas as pl
from jax.experimental.pallas import tpu as pltpu
from jax.sharding import PartitionSpec as P

R = 16
TENANTS = 4
BLOCK = 128
CHUNKS = 2
LANES = 128
VMEM_LIMIT = 56 * 1024 * 1024

ADAPTER_SCALE = 2.0

NT = (((1,), (1,)), ((), ()))
NN = (((1,), (0,)), ((), ()))


def fdot(lhs, rhs, dims):
    return lax.dot_general(lhs, rhs, dims, preferred_element_type=jnp.float32)


def tile_of(width, most):
    tile = most
    while width % tile:
        tile -= LANES
    return tile


def whole(shape):
    return pl.BlockSpec(shape, lambda *_: (0,) * len(shape))


def hidden_kernel(sizes, meta, *refs):
    n_dp, n_t, g, own_t, rc, tile = sizes
    ny = n_t // 2
    pieces, (w_ref, bd_ref, ad_ref, keep_ref, send_ref, x_scr, p_scr) = refs[:n_dp], refs[n_dp:]
    step = pl.program_id(0)
    z, t = meta[0], meta[1]
    y, c = t // 2, t % 2
    width = w_ref.shape[1]
    hidden_width = keep_ref.shape[2] - LANES

    @pl.when(step == 0)
    def _():
        for k in range(n_dp):
            for j in range(g):
                owner = lax.rem(z + (n_dp - k), n_dp) * g + j
                away = jnp.where(owner % 2 == c, 0, ny)
                x_scr[away + lax.rem(owner // 2 + ny - y, ny)] = pieces[k][j]
        x_all = x_scr[...].reshape(n_t * rc, width)
        proj = fdot(x_all, bd_ref[...], NT)
        lane = lax.broadcasted_iota(jnp.int32, (rc, TENANTS * R), 1) // R
        zeros = jnp.zeros((rc, LANES - TENANTS * R), jnp.bfloat16)
        for s in range(n_t):
            owner = lax.rem(y + s % ny, ny) * 2 + (c if s < ny else 1 - c)
            tenant = meta[2 + (owner * own_t) // BLOCK]
            own = jnp.where(lane == tenant, proj[s * rc : (s + 1) * rc], 0.0)
            p_scr[s * rc : (s + 1) * rc, :] = (ADAPTER_SCALE * own).astype(jnp.bfloat16)
            out = keep_ref if s < ny else send_ref
            out[s % ny, :, hidden_width:] = jnp.concatenate([own.astype(jnp.bfloat16), zeros], axis=1)

    acc = fdot(x_scr[...].reshape(n_t * rc, width), w_ref[...], NT) + fdot(p_scr[...], ad_ref[...], NN)
    acc = acc.astype(jnp.bfloat16).reshape(n_t, rc, tile)
    at = pl.ds(pl.multiple_of(step * tile, LANES), tile)
    keep_ref[:, :, at] = acc[:ny]
    send_ref[:, :, at] = acc[ny:]


def hidden_partial(meta, pieces, down_weight, b_down, a_down, n_t, own_t):
    n_dp = len(pieces)
    g, rc, width = pieces[0].shape
    ny = n_t // 2
    hidden_width = down_weight.shape[0]
    tile = tile_of(hidden_width, 512)
    low = TENANTS * R
    out = jax.ShapeDtypeStruct((ny, rc, hidden_width + LANES), jnp.bfloat16)
    return pl.pallas_call(
        functools.partial(hidden_kernel, (n_dp, n_t, g, own_t, rc, tile)),
        out_shape=(out, out),
        grid_spec=pltpu.PrefetchScalarGridSpec(
            num_scalar_prefetch=1,
            grid=(hidden_width // tile,),
            in_specs=[whole((g, rc, width))] * n_dp
            + [
                pl.BlockSpec((tile, width), lambda f, *_: (f, 0)),
                whole((low, width)),
                pl.BlockSpec((low, tile), lambda f, *_: (0, f)),
            ],
            out_specs=[whole(out.shape)] * 2,
            scratch_shapes=[
                pltpu.VMEM((n_t, rc, width), jnp.bfloat16),
                pltpu.VMEM((n_t * rc, low), jnp.bfloat16),
            ],
        ),
        compiler_params=pltpu.CompilerParams(vmem_limit_bytes=VMEM_LIMIT),
        cost_estimate=pl.CostEstimate(
            flops=2 * n_t * rc * width * hidden_width,
            bytes_accessed=2 * width * hidden_width,
            transcendentals=0,
        ),
        name="hidden_partial",
    )(meta, *pieces, down_weight, b_down, a_down)


def act_kernel(keep_ref, pair_ref, far_ref, dgate_ref, dup_ref, out_ref, low_ref):
    width = out_ref.shape[2]
    total = keep_ref[0].astype(jnp.float32) + pair_ref[0].astype(jnp.float32)
    total = total + far_ref[...].astype(jnp.float32)
    low_ref[...] = total[:, width:].astype(jnp.bfloat16)
    hidden_grad = total[:, :width]
    out_ref[0] = (hidden_grad * dgate_ref[...]).astype(jnp.bfloat16)
    out_ref[1] = (hidden_grad * dup_ref[...]).astype(jnp.bfloat16)


def act(keep, pair, far, dgate, dup, q):
    ny, rc, padded = keep.shape
    width = padded - LANES
    return pl.pallas_call(
        act_kernel,
        out_shape=(
            jax.ShapeDtypeStruct((2, rc, width), jnp.bfloat16),
            jax.ShapeDtypeStruct((rc, LANES), jnp.bfloat16),
        ),
        grid=(1,),
        in_specs=[
            whole((1, rc, padded)),
            whole((1, rc, padded)),
            whole((rc, padded)),
            pl.BlockSpec((rc, width), lambda f: (q, 0)),
            pl.BlockSpec((rc, width), lambda f: (q, 0)),
        ],
        out_specs=[whole((2, rc, width)), whole((rc, LANES))],
        compiler_params=pltpu.CompilerParams(vmem_limit_bytes=VMEM_LIMIT),
        cost_estimate=pl.CostEstimate(
            flops=4 * rc * width, bytes_accessed=18 * rc * width, transcendentals=0
        ),
        name="act_grads",
    )(keep, pair, far, dgate, dup)


def owner_of(p, y, c, ny):
    return lax.rem(y + ny - p // 2, ny) * 2 + (c if p % 2 == 0 else 1 - c)


def input_kernel(sizes, meta, *refs):
    n_dp, n_t, g, own_t, rc, tile = sizes
    ny = n_t // 2
    pieces, (gw_ref, uw_ref, b_ref, a_ref), refs = refs[:n_t], refs[n_t : n_t + 4], refs[n_t + 4 :]
    outs, queries, (g_scr, u_scr, q_scr) = refs[:n_dp], refs[n_dp : 2 * n_dp], refs[2 * n_dp :]
    step = pl.program_id(0)
    z, t = meta[0], meta[1]
    y, c = t // 2, t % 2
    width = gw_ref.shape[1]
    rows = n_t * rc

    @pl.when(step == 0)
    def _():
        for p in range(n_t):
            owner = owner_of(p, y, c, ny)
            slot = lax.rem(owner // g + n_dp - z, n_dp) * g + owner % g
            g_scr[slot] = pieces[p][0]
            u_scr[slot] = pieces[p][1]
        q_gate = fdot(g_scr[...].reshape(rows, width), b_ref[...], NT)
        q_up = fdot(u_scr[...].reshape(rows, width), b_ref[...], NT)
        lane = lax.broadcasted_iota(jnp.int32, (rc, 2 * R * TENANTS), 1)
        for r in range(n_dp):
            for j in range(g):
                s = r * g + j
                owner = lax.rem(z + r, n_dp) * g + j
                tenant = meta[2 + (owner * own_t) // BLOCK]
                at = slice(s * rc, (s + 1) * rc)
                query = jnp.where(lane % (2 * R) < R, q_gate[at], q_up[at])
                query = jnp.where(lane // (2 * R) == tenant, query, 0.0)
                q_scr[at, :] = (ADAPTER_SCALE * query).astype(jnp.bfloat16)
                queries[r][j * rc : (j + 1) * rc, :] = query.astype(jnp.bfloat16)

    acc = fdot(g_scr[...].reshape(rows, width), gw_ref[...], NT)
    acc = acc + fdot(u_scr[...].reshape(rows, width), uw_ref[...], NT)
    acc = acc + fdot(q_scr[...], a_ref[...], NN)
    acc = acc.astype(jnp.bfloat16)
    at = pl.ds(pl.multiple_of(step * tile, LANES), tile)
    for r in range(n_dp):
        outs[r][:, at] = acc[r * g * rc : (r + 1) * g * rc]


def input_partial(meta, pieces, gate_weight, up_weight, b_gu, a_gu, n_dp, own_t):
    n_t = len(pieces)
    _, rc, hidden_width = pieces[0].shape
    g = n_t // n_dp
    width = gate_weight.shape[0]
    tile = tile_of(width, 256)
    low = 2 * R * TENANTS
    rows = n_t * rc
    outs = [jax.ShapeDtypeStruct((g * rc, width), jnp.bfloat16)] * n_dp
    queries = [jax.ShapeDtypeStruct((g * rc, low), jnp.bfloat16)] * n_dp
    result = pl.pallas_call(
        functools.partial(input_kernel, (n_dp, n_t, g, own_t, rc, tile)),
        out_shape=outs + queries,
        grid_spec=pltpu.PrefetchScalarGridSpec(
            num_scalar_prefetch=1,
            grid=(width // tile,),
            in_specs=[whole((2, rc, hidden_width))] * n_t
            + [
                pl.BlockSpec((tile, hidden_width), lambda d, *_: (d, 0)),
                pl.BlockSpec((tile, hidden_width), lambda d, *_: (d, 0)),
                whole((low, hidden_width)),
                pl.BlockSpec((low, tile), lambda d, *_: (0, d)),
            ],
            out_specs=[whole(o.shape) for o in outs + queries],
            scratch_shapes=[
                pltpu.VMEM((n_t, rc, hidden_width), jnp.bfloat16),
                pltpu.VMEM((n_t, rc, hidden_width), jnp.bfloat16),
                pltpu.VMEM((rows, low), jnp.bfloat16),
            ],
        ),
        compiler_params=pltpu.CompilerParams(vmem_limit_bytes=VMEM_LIMIT),
        cost_estimate=pl.CostEstimate(
            flops=4 * rows * width * hidden_width,
            bytes_accessed=4 * width * hidden_width,
            transcendentals=0,
        ),
        name="input_partial",
    )(meta, *pieces, gate_weight, up_weight, b_gu, a_gu)
    return result[:n_dp], result[n_dp:]


def outer_kernel(owners, count, meta, *refs):
    pieces, left_ref, out_ref = refs[:count], refs[count], refs[count + 1]
    for layer in range(out_ref.shape[0]):
        total = None
        for k in range(count):
            owner, q, layer_at = owners(k, meta, layer)
            term = fdot(left_ref[layer, owner, q], pieces[k][layer_at], NN)
            total = term if total is None else total + term
        out_ref[layer] = ADAPTER_SCALE * total


def outer(meta, pieces, left, owners, layers, name):
    count = len(pieces)
    depth, rc, width = pieces[0].shape
    tile = tile_of(width, 512)
    rows = left.shape[3]
    return pl.pallas_call(
        functools.partial(outer_kernel, owners, count),
        out_shape=jax.ShapeDtypeStruct((layers, rows, width), jnp.float32),
        grid_spec=pltpu.PrefetchScalarGridSpec(
            num_scalar_prefetch=1,
            grid=(width // tile,),
            in_specs=[pl.BlockSpec((depth, rc, tile), lambda f, *_: (0, 0, f))] * count
            + [whole(left.shape)],
            out_specs=pl.BlockSpec((layers, rows, tile), lambda f, *_: (0, 0, f)),
        ),
        compiler_params=pltpu.CompilerParams(vmem_limit_bytes=VMEM_LIMIT),
        cost_estimate=pl.CostEstimate(
            flops=2 * count * layers * rows * rc * width,
            bytes_accessed=2 * count * depth * rc * width + 4 * layers * rows * width,
            transcendentals=0,
        ),
        name=name,
    )(meta, *pieces, left)


def ring(n, by):
    return [(k, (k + by) % n) for k in range(n)]


def add32(*terms):
    return sum(term.astype(jnp.float32) for term in terms)


def spread(tenants, parts):
    heads = jnp.arange(TENANTS, dtype=jnp.int32)
    total = 0.0
    for tenant, part in zip(tenants, parts):
        chosen = (heads == tenant).astype(jnp.float32)[:, None, None]
        total = total + chosen * part.astype(jnp.float32)[None]
    return ADAPTER_SCALE * total


def per_device(
    layer_input,
    out_grad,
    gate_pre,
    up_pre,
    adapter_acts,
    gate_weight,
    up_weight,
    down_weight,
    adapter_a_gu,
    adapter_b_gu,
    adapter_a_down,
    adapter_b_down,
    block_tenant,
):
    n_dp, n_t = lax.axis_size("dp"), lax.axis_size("tensor")
    ny = n_t // 2
    z, t = lax.axis_index("dp"), lax.axis_index("tensor")
    y, c = t // 2, t % 2
    own_rows, width = out_grad.shape
    own_t, hidden_width = gate_pre.shape
    tokens = adapter_acts.shape[0]
    g = own_rows // own_t
    rc = own_t // CHUNKS
    assert own_rows == BLOCK and g * own_t == own_rows and n_t == 2 * ny and n_t == g * n_dp

    meta = jnp.concatenate([jnp.stack([z, t]).astype(jnp.int32), block_tenant])
    b_down = adapter_b_down.reshape(TENANTS * R, width)
    a_down = jnp.transpose(adapter_a_down, (0, 2, 1)).reshape(TENANTS * R, hidden_width)
    b_gu = adapter_b_gu.reshape(TENANTS * 2 * R, hidden_width)
    a_gu = jnp.transpose(adapter_a_gu, (0, 2, 1)).reshape(TENANTS * 2 * R, width)

    pair = [(k, k ^ 1) for k in range(n_t)]
    y_next = ring(n_t, 2)
    z_next = ring(n_dp, 1)

    grads = []
    for q in range(CHUNKS):
        piece = out_grad.reshape(g, own_t, width)[:, q * rc : (q + 1) * rc]
        pieces = [piece]
        for _ in range(n_dp - 1):
            piece = lax.ppermute(piece, "dp", z_next)
            pieces.append(piece)
        grads.append(pieces)

    gate_value = gate_pre.astype(jnp.float32)
    up_value = up_pre.astype(jnp.float32)
    sigmoid_value = jax.nn.sigmoid(gate_value)
    hidden = (gate_value * sigmoid_value * up_value).astype(jnp.bfloat16)
    dgate = up_value * sigmoid_value * (1.0 + gate_value * (1.0 - sigmoid_value))
    dup = gate_value * sigmoid_value
    onehot = (
        jnp.arange(TENANTS, dtype=jnp.int32)[:, None] == jnp.repeat(block_tenant, BLOCK)[None, :]
    ).astype(jnp.bfloat16)
    acts = adapter_acts.T.reshape(3, 1, R, tokens) * onehot[None, :, None, :]
    acts = acts.reshape(3, TENANTS * R, n_t, CHUNKS, rc).transpose(0, 2, 3, 1, 4)

    gathered, lows = [], []
    for q in range(CHUNKS):
        keep, send = hidden_partial(meta, grads[q], down_weight, b_down, a_down, n_t, own_t)
        other = lax.ppermute(send, "tensor", pair)
        message = add32(keep[ny - 1], other[ny - 1]).astype(jnp.bfloat16)
        for s in range(ny - 1):
            far = lax.ppermute(message, "tensor", y_next)
            if s < ny - 2:
                message = add32(keep[ny - 2 - s], other[ny - 2 - s], far).astype(jnp.bfloat16)
        own, low = act(keep, other, far, dgate, dup, q)
        lows.append(low)
        pieces = [own, lax.ppermute(own, "tensor", pair)]
        for _ in range(ny - 1):
            own = lax.ppermute(own, "tensor", y_next)
            pieces += [own, lax.ppermute(own, "tensor", pair)]
        gathered.append(pieces)

    low = jnp.concatenate(lows, axis=0)[:, : TENANTS * R]
    a_part = lax.dot_general(low, hidden, (((0,), (0,)), ((), ())), preferred_element_type=jnp.float32)
    a_part = a_part.reshape(TENANTS, R, hidden_width).sum(0).astype(jnp.bfloat16)
    column = [a_part] + [lax.ppermute(a_part, "tensor", ring(n_t, 2 * s)) for s in range(1, ny)]
    beside = lax.ppermute(jnp.concatenate(column, axis=0), "tensor", pair)
    a_parts = []
    for s in range(ny):
        a_parts += [column[s], beside[s * R : (s + 1) * R]]
    a_tenants = [block_tenant[(owner_of(p, y, c, ny) * own_t) // BLOCK] for p in range(n_t)]
    grad_a_down = spread(a_tenants, a_parts).transpose(0, 2, 1)

    input_parts, in_parts = [], 0.0
    for q in range(CHUNKS):
        outs, queries = input_partial(
            meta, gathered[q], gate_weight, up_weight, b_gu, a_gu, n_dp, own_t
        )
        query = add32(
            queries[0], *[lax.ppermute(queries[r], "dp", ring(n_dp, r)) for r in range(1, n_dp)]
        ).astype(jnp.bfloat16)
        rows_in = layer_input.reshape(g, own_t, width)[:, q * rc : (q + 1) * rc].reshape(g * rc, width)
        part = lax.dot_general(query, rows_in, (((0,), (0,)), ((), ())), preferred_element_type=jnp.float32)
        in_parts = in_parts + part.reshape(TENANTS, 2 * R, width).sum(0)
        message = outs[n_dp - 1]
        for s in range(n_dp - 1):
            message = lax.ppermute(message, "dp", z_next)
            message = add32(message, outs[n_dp - 2 - s]).astype(jnp.bfloat16)
        input_parts.append(message.reshape(g, rc, width))
    block_input_grad = jnp.concatenate(input_parts, axis=1).reshape(own_rows, width)

    in_part = in_parts.astype(jnp.bfloat16)
    in_all = [in_part] + [lax.ppermute(in_part, "dp", ring(n_dp, r)) for r in range(1, n_dp)]
    in_tenants = [block_tenant[lax.rem(z + n_dp - r, n_dp)] for r in range(n_dp)]
    grad_a_gu = spread(in_tenants, in_all).transpose(0, 2, 1)

    def grad_owner(k, meta, layer):
        q, k = divmod(k, n_dp * g)
        k, j = divmod(k, g)
        return lax.rem(meta[0] + (n_dp - k), n_dp) * g + j, q, 0

    def gathered_owner(k, meta, layer):
        q, p = divmod(k, n_t)
        return owner_of(p, meta[1] // 2, meta[1] % 2, ny), q, layer

    x_pieces = [x[j : j + 1] for pieces in grads for x in pieces for j in range(g)]
    grad_b_down = outer(meta, x_pieces, acts[2:], grad_owner, 1, "down_outer")
    grad_b_down = grad_b_down.reshape(TENANTS, R, width)
    gu_pieces = [piece for pieces in gathered for piece in pieces]
    grad_b_gu = outer(meta, gu_pieces, acts[:2], gathered_owner, 2, "gate_up_outer")
    grad_b_gu = grad_b_gu.reshape(2, TENANTS, R, hidden_width).transpose(1, 0, 2, 3)
    grad_b_gu = grad_b_gu.reshape(TENANTS, 2 * R, hidden_width)
    return (block_input_grad, grad_a_gu, grad_b_gu, grad_a_down, grad_b_down)


def solution(mesh):
    placed = (
        P(("groups", "dp"), "tensor"),
        P(("groups", "dp"), "tensor"),
        P(("groups", "tensor"), "dp"),
        P(("groups", "tensor"), "dp"),
        P("groups", None),
        P("tensor", "dp"),
        P("tensor", "dp"),
        P("dp", "tensor"),
        P(None, "tensor", None),
        P(None, None, "dp"),
        P(None, "dp", None),
        P(None, None, "tensor"),
        P("groups"),
    )
    return jax.shard_map(
        per_device,
        mesh=mesh,
        in_specs=placed,
        out_specs=(
            P(("groups", "dp"), "tensor"),
            P("groups", "tensor", None),
            P("groups", None, "dp"),
            P("groups", "dp", None),
            P("groups", None, "tensor"),
        ),
        check_vma=False,
    )
```

profile of v0, /device:TPU:0, one launch (start us, length us, event | category | flops | bytes accessed | tf_op | source)
XLA Modules:
  0.0 261.7 jit_solution(17135275140954494979)
XLA Ops:
  1.7 3.1 %collective-permute-start = (bf16[1,64,2048]{2,1,0:T(8,128)(2,1)S(1)}, bf16[1,64,2048]{2,1,0:T(8,128)(2,1)S(1)}, u32[]{:S(2)}, u32[]{:S(2)}) collective-permute-start(bf16[1,64,2048]{2,1,0:T(8,128)(2,1)S(1)} %get-tuple-element.57.refs_0_), channel_id=1, source_target_pairs={{0,1},{1,2},{2,3},{3,0},{4,5},{5,6},{6,7},{7,4},{8,9},{9,10},{10,1... | collective-permute-start | bytes 786440 | tf_op jit(solution)/shard_map/ppermute | solution.py:326
  6.4 7.6 %collective-permute-done.refs_1_ = bf16[1,64,2048]{2,1,0:T(8,128)(2,1)S(1)} collective-permute-done((bf16[1,64,2048]{2,1,0:T(8,128)(2,1)S(1)}, bf16[1,64,2048]{2,1,0:T(8,128)(2,1)S(1)}, u32[]{:S(2)}, u32[]{:S(2)}) %collective-permute-start) | collective-permute-done | bytes 262176 | tf_op jit(solution)/shard_map/ppermute | solution.py:326
  14.0 5.6 %collective-permute-done.11.refs_1_.refs_5_ = bf16[1,64,2048]{2,1,0:T(8,128)(2,1)S(1)} collective-permute-done((bf16[1,64,2048]{2,1,0:T(8,128)(2,1)S(1)}, bf16[1,64,2048]{2,1,0:T(8,128)(2,1)S(1)}, u32[]{:S(2)}, u32[]{:S(2)}) %collective-permute-start.11) | collective-permute-done | bytes 262176 | tf_op jit(solution)/shard_map/ppermute | solution.py:326
  19.6 5.6 %collective-permute-done.1.refs_2_ = bf16[1,64,2048]{2,1,0:T(8,128)(2,1)S(1)} collective-permute-done((bf16[1,64,2048]{2,1,0:T(8,128)(2,1)S(1)}, bf16[1,64,2048]{2,1,0:T(8,128)(2,1)S(1)}, u32[]{:S(2)}, u32[]{:S(2)}) %collective-permute-start.1) | collective-permute-done | bytes 262176 | tf_op jit(solution)/shard_map/ppermute | solution.py:326
  26.5 4.3 %collective-permute-done.12.refs_2_.refs_6_ = bf16[1,64,2048]{2,1,0:T(8,128)(2,1)S(1)} collective-permute-done((bf16[1,64,2048]{2,1,0:T(8,128)(2,1)S(1)}, bf16[1,64,2048]{2,1,0:T(8,128)(2,1)S(1)}, u32[]{:S(2)}, u32[]{:S(2)}) %collective-permute-start.12) | collective-permute-done | bytes 262176 | tf_op jit(solution)/shard_map/ppermute | solution.py:326
  30.8 5.6 %collective-permute-done.2.refs_3_ = bf16[1,64,2048]{2,1,0:T(8,128)(2,1)S(1)} collective-permute-done((bf16[1,64,2048]{2,1,0:T(8,128)(2,1)S(1)}, bf16[1,64,2048]{2,1,0:T(8,128)(2,1)S(1)}, u32[]{:S(2)}, u32[]{:S(2)}) %collective-permute-start.2) | collective-permute-done | bytes 262176 | tf_op jit(solution)/shard_map/ppermute | solution.py:326
  37.1 12.5 %hidden_partial.2 = (bf16[2,64,3712]{2,1,0:T(8,128)(2,1)}, bf16[2,64,3712]{2,1,0:T(8,128)(2,1)}) custom-call(s32[6]{0:T(128)} %pad_add_fusion.meta, bf16[1,64,2048]{2,1,0:T(8,128)(2,1)} %copy-done.8, bf16[1,64,2048]{2,1,0:T(8,128)(2,1)} %copy-done.13, bf16[1,64,2048]{2,1,0:T(8,128)(2,1)} %copy-done.15, bf16[1,64,2048]{2,1,0:T(8,128)(2,1)} %copy-done.17, ...), custom_call_target="tpu_custom_call" | custom-call | flops 3758096384 | bytes 14680064 | tf_op jit(solution)/shard_map/hidden_partial/pallas_call | solution.py:82
  53.3 12.3 %hidden_partial.3 = (bf16[2,64,3712]{2,1,0:T(8,128)(2,1)}, bf16[2,64,3712]{2,1,0:T(8,128)(2,1)}) custom-call(s32[6]{0:T(128)} %pad_add_fusion.meta, bf16[1,64,2048]{2,1,0:T(8,128)(2,1)} %copy-done.9, bf16[1,64,2048]{2,1,0:T(8,128)(2,1)} %copy-done.14, bf16[1,64,2048]{2,1,0:T(8,128)(2,1)} %copy-done.16, bf16[1,64,2048]{2,1,0:T(8,128)(2,1)} %copy-done.18, ...), custom_call_target="tpu_custom_call" | custom-call | flops 3758096384 | bytes 14680064 | tf_op jit(solution)/shard_map/hidden_partial/pallas_call | solution.py:82
  81.1 4.8 %down_outer.1 = f32[1,64,2048]{2,1,0:T(8,128)} custom-call(s32[6]{0:T(128)} %pad_add_fusion.meta, bf16[1,64,2048]{2,1,0:T(8,128)(2,1)} %copy-done.8, bf16[1,64,2048]{2,1,0:T(8,128)(2,1)} %copy-done.13, bf16[1,64,2048]{2,1,0:T(8,128)(2,1)} %copy-done.15, bf16[1,64,2048]{2,1,0:T(8,128)(2,1)} %copy-done.17, bf16[1,64,2048]{2,1,0:T(8,128)(2,1)} %copy-done.9, ...), custom_call_target="tpu_custom_call" | custom-call | flops 134217728 | bytes 2621440 | tf_op jit(solution)/shard_map/down_outer/pallas_call | solution.py:248
  85.9 5.4 %collective-permute-done.15.far_ref = bf16[64,3712]{1,0:T(8,128)(2,1)S(1)} collective-permute-done((bf16[64,3712]{1,0:T(8,128)(2,1)S(1)}, bf16[64,3712]{1,0:T(8,128)(2,1)S(1)}, u32[]{:S(2)}, u32[]{:S(2)}) %collective-permute-start.15) | collective-permute-done | bytes 475168 | tf_op jit(solution)/shard_map/ppermute | solution.py:348
  92.1 3.1 %act_grads.3 = (bf16[2,64,3584]{2,1,0:T(8,128)(2,1)}, bf16[64,128]{1,0:T(8,128)(2,1)}) custom-call(bf16[2,64,3712]{2,1,0:T(8,128)(2,1)} %get-tuple-element.36.keep_ref, bf16[2,64,3712]{2,1,0:T(8,128)(2,1)} %collective-permute-done.14.pair_ref, bf16[64,3712]{1,0:T(8,128)(2,1)} %copy-done.26, f32[128,3584]{1,0:T(8,128)} %get-tuple-element.56.dgate_ref, ...), custom_call_target="tpu_custom_call" | custom-call | flops 917504 | bytes 4128768 | tf_op jit(solution)/shard_map/act_grads/pallas_call | solution.py:123
  95.3 3.2 %act_grads.2 = (bf16[2,64,3584]{2,1,0:T(8,128)(2,1)}, bf16[64,128]{1,0:T(8,128)(2,1)}) custom-call(bf16[2,64,3712]{2,1,0:T(8,128)(2,1)} %get-tuple-element.29.keep_ref, bf16[2,64,3712]{2,1,0:T(8,128)(2,1)} %copy-done.11, bf16[64,3712]{1,0:T(8,128)(2,1)} %collective-permute-done.4.far_ref, f32[128,3584]{1,0:T(8,128)} %get-tuple-element.56.dgate_ref, ...), custom_call_target="tpu_custom_call" | custom-call | flops 917504 | bytes 4128768 | tf_op jit(solution)/shard_map/act_grads/pallas_call | solution.py:123
  106.4 19.6 %collective-permute-done.6.refs_2_ = bf16[2,64,3584]{2,1,0:T(8,128)(2,1)S(1)} collective-permute-done((bf16[2,64,3584]{2,1,0:T(8,128)(2,1)S(1)}, bf16[2,64,3584]{2,1,0:T(8,128)(2,1)S(1)}, u32[]{:S(2)}, u32[]{:S(2)}) %collective-permute-start.6) | collective-permute-done | bytes 917536 | tf_op jit(solution)/shard_map/ppermute | solution.py:355
  126.0 18.1 %collective-permute-done.17.refs_2_.refs_6_ = bf16[2,64,3584]{2,1,0:T(8,128)(2,1)S(1)} collective-permute-done((bf16[2,64,3584]{2,1,0:T(8,128)(2,1)S(1)}, bf16[2,64,3584]{2,1,0:T(8,128)(2,1)S(1)}, u32[]{:S(2)}, u32[]{:S(2)}) %collective-permute-start.17) | collective-permute-done | bytes 917536 | tf_op jit(solution)/shard_map/ppermute | solution.py:355
  146.1 19.3 %input_partial.2 = (bf16[64,2048]{1,0:T(8,128)(2,1)}, bf16[64,2048]{1,0:T(8,128)(2,1)}, bf16[64,2048]{1,0:T(8,128)(2,1)}, bf16[64,2048]{1,0:T(8,128)(2,1)}, bf16...) custom-call(s32[6]{0:T(128)} %pad_add_fusion.meta, ...), custom_call_target="tpu_custom_call" | custom-call | flops 7516192768 | bytes 29360128 | tf_op jit(solution)/shard_map/input_partial/pallas_call | solution.py:201
  171.3 19.4 %input_partial.3 = (bf16[64,2048]{1,0:T(8,128)(2,1)}, bf16[64,2048]{1,0:T(8,128)(2,1)}, bf16[64,2048]{1,0:T(8,128)(2,1)}, bf16[64,2048]{1,0:T(8,128)(2,1)}, bf16...) custom-call(s32[6]{0:T(128)} %pad_add_fusion.meta, ...), custom_call_target="tpu_custom_call" | custom-call | flops 7516192768 | bytes 29360128 | tf_op jit(solution)/shard_map/input_partial/pallas_call | solution.py:201
  201.3 8.8 %gate_up_outer.1 = f32[2,64,3584]{2,1,0:T(8,128)} custom-call(s32[6]{0:T(128)} %pad_add_fusion.meta, bf16[2,64,3584]{2,1,0:T(8,128)(2,1)} %get-tuple-element.31.refs_0_, bf16[2,64,3584]{2,1,0:T(8,128)(2,1)} %copy-done.5, bf16[2,64,3584]{2,1,0:T(8,128)(2,1)} %copy-done.2, bf16[2,64,3584]{2,1,0:T(8,128)(2,1)} %copy-done.6, ...), custom_call_target="tpu_custom_call" | custom-call | flops 469762048 | bytes 9175040 | tf_op jit(solution)/shard_map/gate_up_outer/pallas_call | solution.py:248
  213.0 3.6 %collective-permute-start.8 = (bf16[64,2048]{1,0:T(8,128)(2,1)S(1)}, bf16[64,2048]{1,0:T(8,128)(2,1)S(1)}, u32[]{:S(2)}, u32[]{:S(2)}) collective-permute-start(bf16[64,2048]{1,0:T(8,128)(2,1)S(1)} %copy-done.44), channel_id=1, source_target_pairs={{0,1},{1,2},{2,3},{3,0},{4,5},{5,6},{6,7},{7,4},{8,9},{9,10},{10,1... | collective-permute-start | bytes 786440 | tf_op jit(solution)/shard_map/ppermute | solution.py:383
  217.2 3.3 %collective-permute-start.30 = (bf16[32,2048]{1,0:T(8,128)(2,1)S(1)}, bf16[32,2048]{1,0:T(8,128)(2,1)S(1)}, u32[]{:S(2)}, u32[]{:S(2)}) collective-permute-start(bf16[32,2048]{1,0:T(8,128)(2,1)S(1)} %get-tuple-element.54), channel_id=1, source_target_pairs={{0,3},{1,0},{2,1},{3,2},{4,7},{5,4},{6,5},{7,6},{8,11},{9,8},{10,9... | collective-permute-start | bytes 393224 | tf_op jit(solution)/shard_map/ppermute | solution.py:389
  220.5 10.6 %collective-permute-done.28 = bf16[32,2048]{1,0:T(8,128)(2,1)S(1)} collective-permute-done((bf16[32,2048]{1,0:T(8,128)(2,1)S(1)}, bf16[32,2048]{1,0:T(8,128)(2,1)S(1)}, u32[]{:S(2)}, u32[]{:S(2)}) %collective-permute-start.28) | collective-permute-done | bytes 131104 | tf_op jit(solution)/shard_map/ppermute | solution.py:389
  235.3 9.6 %collective-permute-done.9 = bf16[64,2048]{1,0:T(8,128)(2,1)S(1)} collective-permute-done((bf16[64,2048]{1,0:T(8,128)(2,1)S(1)}, bf16[64,2048]{1,0:T(8,128)(2,1)S(1)}, u32[]{:S(2)}, u32[]{:S(2)}) %collective-permute-start.9) | collective-permute-done | bytes 262176 | tf_op jit(solution)/shard_map/ppermute | solution.py:383
  245.1 5.5 %collective-permute-done.20 = bf16[64,2048]{1,0:T(8,128)(2,1)S(1)} collective-permute-done((bf16[64,2048]{1,0:T(8,128)(2,1)S(1)}, bf16[64,2048]{1,0:T(8,128)(2,1)S(1)}, u32[]{:S(2)}, u32[]{:S(2)}) %collective-permute-start.20) | collective-permute-done | bytes 262176 | tf_op jit(solution)/shard_map/ppermute | solution.py:383
  250.7 5.5 %collective-permute-done.10 = bf16[64,2048]{1,0:T(8,128)(2,1)S(1)} collective-permute-done((bf16[64,2048]{1,0:T(8,128)(2,1)S(1)}, bf16[64,2048]{1,0:T(8,128)(2,1)S(1)}, u32[]{:S(2)}, u32[]{:S(2)}) %collective-permute-start.10) | collective-permute-done | bytes 262176 | tf_op jit(solution)/shard_map/ppermute | solution.py:383
  256.2 4.5 %collective-permute-done.21 = bf16[64,2048]{1,0:T(8,128)(2,1)S(1)} collective-permute-done((bf16[64,2048]{1,0:T(8,128)(2,1)S(1)}, bf16[64,2048]{1,0:T(8,128)(2,1)S(1)}, u32[]{:S(2)}, u32[]{:S(2)}) %collective-permute-start.21) | collective-permute-done | bytes 262176 | tf_op jit(solution)/shard_map/ppermute | solution.py:383
  (190 shorter events, 59.3 us)
Async XLA Ops:
  1.7 12.2 %collective-permute-start = (bf16[1,64,2048]{2,1,0:T(8,128)(2,1)S(1)}, bf16[1,64,2048]{2,1,0:T(8,128)(2,1)S(1)}, u32[]{:S(2)}, u32[]{:S(2)}) collective-permute-start(bf16[1,64,2048]{2,1,0:T(8,128)(2,1)S(1)} %get-tuple-element.57.refs_0_), channel_id=1, source_target_pairs={{0,1},{1,2},{2,3},{3,0},{4,5},{5,6},{6,7},{7,4},{8,9},{9,10},{10,1... | collective-permute-start | bytes 786440 | tf_op jit(solution)/shard_map/ppermute | solution.py:326
  4.8 14.8 %collective-permute-start.11 = (bf16[1,64,2048]{2,1,0:T(8,128)(2,1)S(1)}, bf16[1,64,2048]{2,1,0:T(8,128)(2,1)S(1)}, u32[]{:S(2)}, u32[]{:S(2)}) collective-permute-start(bf16[1,64,2048]{2,1,0:T(8,128)(2,1)S(1)} %get-tuple-element.58.refs_0_.refs_4_), channel_id=1, source_target_pairs={{0,1},{1,2},{2,3},{3,0},{4,5},{5,6},{6,7},{7,4},{8,9},{9,10},{10,1... | collective-permute-start | bytes 786440 | tf_op jit(solution)/shard_map/ppermute | solution.py:326
  19.6 11.2 %collective-permute-start.12 = (bf16[1,64,2048]{2,1,0:T(8,128)(2,1)S(1)}, bf16[1,64,2048]{2,1,0:T(8,128)(2,1)S(1)}, u32[]{:S(2)}, u32[]{:S(2)}) collective-permute-start(bf16[1,64,2048]{2,1,0:T(8,128)(2,1)S(1)} %collective-permute-done.11.refs_1_.refs_5_), channel_id=1, source_target_pairs={{0,1},{1,2},{2,3},{3,0},{4,5},{5,6},{6,7},{7,4},{8,9},{9,10},{10,1... | collective-permute-start | bytes 786440 | tf_op jit(solution)/shard_map/ppermute | solution.py:326
  25.2 11.2 %collective-permute-start.2 = (bf16[1,64,2048]{2,1,0:T(8,128)(2,1)S(1)}, bf16[1,64,2048]{2,1,0:T(8,128)(2,1)S(1)}, u32[]{:S(2)}, u32[]{:S(2)}) collective-permute-start(bf16[1,64,2048]{2,1,0:T(8,128)(2,1)S(1)} %collective-permute-done.1.refs_2_), channel_id=1, source_target_pairs={{0,1},{1,2},{2,3},{3,0},{4,5},{5,6},{6,7},{7,4},{8,9},{9,10},{10,1... | collective-permute-start | bytes 786440 | tf_op jit(solution)/shard_map/ppermute | solution.py:326
  30.8 21.8 %collective-permute-start.13 = (bf16[1,64,2048]{2,1,0:T(8,128)(2,1)S(1)}, bf16[1,64,2048]{2,1,0:T(8,128)(2,1)S(1)}, u32[]{:S(2)}, u32[]{:S(2)}) collective-permute-start(bf16[1,64,2048]{2,1,0:T(8,128)(2,1)S(1)} %collective-permute-done.12.refs_2_.refs_6_), channel_id=1, source_target_pairs={{0,1},{1,2},{2,3},{3,0},{4,5},{5,6},{6,7},{7,4},{8,9},{9,10},{10,1... | collective-permute-start | bytes 786440 | tf_op jit(solution)/shard_map/ppermute | solution.py:326
  49.7 17.5 %collective-permute-start.3 = (bf16[2,64,3712]{2,1,0:T(8,128)(2,1)}, bf16[2,64,3712]{2,1,0:T(8,128)(2,1)S(1)}, u32[]{:S(2)}, u32[]{:S(2)}) collective-permute-start(bf16[2,64,3712]{2,1,0:T(8,128)(2,1)} %get-tuple-element.30), channel_id=1, source_target_pairs={{0,4},{4,0},{8,12},{12,8},{1,5},{5,1},{9,13},{13,9},{2,6},{6,2},{1... | collective-permute-start | bytes 2850824 | tf_op jit(solution)/shard_map/ppermute | solution.py:345
  68.1 27.1 %collective-permute-start.4 = (bf16[64,3712]{1,0:T(8,128)(2,1)}, bf16[64,3712]{1,0:T(8,128)(2,1)}, u32[]{:S(2)}, u32[]{:S(2)}) collective-permute-start(bf16[64,3712]{1,0:T(8,128)(2,1)} %fusion.8), channel_id=1, source_target_pairs={{0,8},{4,12},{8,0},{12,4},{1,9},{5,13},{9,1},{13,5},{2,10},{6,14},... | collective-permute-start | bytes 1425416 | tf_op jit(solution)/shard_map/ppermute | solution.py:348
  71.1 20.3 %collective-permute-start.15 = (bf16[64,3712]{1,0:T(8,128)(2,1)S(1)}, bf16[64,3712]{1,0:T(8,128)(2,1)S(1)}, u32[]{:S(2)}, u32[]{:S(2)}) collective-permute-start(bf16[64,3712]{1,0:T(8,128)(2,1)S(1)} %fusion.9), channel_id=1, source_target_pairs={{0,8},{4,12},{8,0},{12,4},{1,9},{5,13},{9,1},{13,5},{2,10},{6,14},... | collective-permute-start | bytes 1425416 | tf_op jit(solution)/shard_map/ppermute | solution.py:348
  102.0 23.9 %collective-permute-start.6 = (bf16[2,64,3584]{2,1,0:T(8,128)(2,1)S(1)}, bf16[2,64,3584]{2,1,0:T(8,128)(2,1)S(1)}, u32[]{:S(2)}, u32[]{:S(2)}) collective-permute-start(bf16[2,64,3584]{2,1,0:T(8,128)(2,1)S(1)} %copy-done.1), channel_id=1, source_target_pairs={{0,8},{4,12},{8,0},{12,4},{1,9},{5,13},{9,1},{13,5},{2,10},{6,14},... | collective-permute-start | bytes 2752520 | tf_op jit(solution)/shard_map/ppermute | solution.py:355
  102.3 41.7 %collective-permute-start.17 = (bf16[2,64,3584]{2,1,0:T(8,128)(2,1)S(1)}, bf16[2,64,3584]{2,1,0:T(8,128)(2,1)S(1)}, u32[]{:S(2)}, u32[]{:S(2)}) collective-permute-start(bf16[2,64,3584]{2,1,0:T(8,128)(2,1)S(1)} %copy-done), channel_id=1, source_target_pairs={{0,8},{4,12},{8,0},{12,4},{1,9},{5,13},{9,1},{13,5},{2,10},{6,14},... | collective-permute-start | bytes 2752520 | tf_op jit(solution)/shard_map/ppermute | solution.py:355
  104.2 65.2 %collective-permute-start.16 = (bf16[2,64,3584]{2,1,0:T(8,128)(2,1)S(1)}, bf16[2,64,3584]{2,1,0:T(8,128)(2,1)S(1)}, u32[]{:S(2)}, u32[]{:S(2)}) collective-permute-start(bf16[2,64,3584]{2,1,0:T(8,128)(2,1)S(1)} %copy-done), channel_id=1, source_target_pairs={{0,4},{4,0},{8,12},{12,8},{1,5},{5,1},{9,13},{13,9},{2,6},{6,2},{1... | collective-permute-start | bytes 2752520 | tf_op jit(solution)/shard_map/ppermute | solution.py:353
  104.2 40.7 %collective-permute-start.5 = (bf16[2,64,3584]{2,1,0:T(8,128)(2,1)S(1)}, bf16[2,64,3584]{2,1,0:T(8,128)(2,1)S(1)}, u32[]{:S(2)}, u32[]{:S(2)}) collective-permute-start(bf16[2,64,3584]{2,1,0:T(8,128)(2,1)S(1)} %copy-done.1), channel_id=1, source_target_pairs={{0,4},{4,0},{8,12},{12,8},{1,5},{5,1},{9,13},{13,9},{2,6},{6,2},{1... | collective-permute-start | bytes 2752520 | tf_op jit(solution)/shard_map/ppermute | solution.py:353
  106.3 37.8 %collective-permute-start.32 = (bf16[32,3584]{1,0:T(8,128)(2,1)S(1)}, bf16[32,3584]{1,0:T(8,128)(2,1)S(1)}, u32[]{:S(2)}, u32[]{:S(2)}) collective-permute-start(bf16[32,3584]{1,0:T(8,128)(2,1)S(1)} %pad_maximum_fusion), channel_id=1, source_target_pairs={{0,4},{4,0},{8,12},{12,8},{1,5},{5,1},{9,13},{13,9},{2,6},{6,2},{1... | collective-permute-start | bytes 688136 | tf_op jit(solution)/shard_map/ppermute | solution.py:363
  126.0 18.9 %collective-permute-start.7 = (bf16[2,64,3584]{2,1,0:T(8,128)(2,1)S(1)}, bf16[2,64,3584]{2,1,0:T(8,128)(2,1)S(1)}, u32[]{:S(2)}, u32[]{:S(2)}) collective-permute-start(bf16[2,64,3584]{2,1,0:T(8,128)(2,1)S(1)} %collective-permute-done.6.refs_2_), channel_id=1, source_target_pairs={{0,4},{4,0},{8,12},{12,8},{1,5},{5,1},{9,13},{13,9},{2,6},{6,2},{1... | collective-permute-start | bytes 2752520 | tf_op jit(solution)/shard_map/ppermute | solution.py:356
  144.1 25.3 %collective-permute-start.18 = (bf16[2,64,3584]{2,1,0:T(8,128)(2,1)S(1)}, bf16[2,64,3584]{2,1,0:T(8,128)(2,1)S(1)}, u32[]{:S(2)}, u32[]{:S(2)}) collective-permute-start(bf16[2,64,3584]{2,1,0:T(8,128)(2,1)S(1)} %collective-permute-done.17.refs_2_.refs_6_), channel_id=1, source_target_pairs={{0,4},{4,0},{8,12},{12,8},{1,5},{5,1},{9,13},{13,9},{2,6},{6,2},{1... | collective-permute-start | bytes 2752520 | tf_op jit(solution)/shard_map/ppermute | solution.py:356
  165.5 27.5 %collective-permute-start.22 = (bf16[64,128]{1,0:T(8,128)(2,1)}, bf16[64,128]{1,0:T(8,128)(2,1)S(1)}, u32[]{:S(2)}, u32[]{:S(2)}) collective-permute-start(bf16[64,128]{1,0:T(8,128)(2,1)} %get-tuple-element.44), channel_id=1, source_target_pairs={{0,1},{1,2},{2,3},{3,0},{4,5},{5,6},{6,7},{7,4},{8,9},{9,10},{10,1... | collective-permute-start | bytes 49160 | tf_op jit(solution)/shard_map/ppermute | solution.py:376
  165.5 30.2 %collective-permute-start.23 = (bf16[64,128]{1,0:T(8,128)(2,1)}, bf16[64,128]{1,0:T(8,128)(2,1)S(1)}, u32[]{:S(2)}, u32[]{:S(2)}) collective-permute-start(bf16[64,128]{1,0:T(8,128)(2,1)} %get-tuple-element.45), channel_id=1, source_target_pairs={{0,2},{1,3},{2,0},{3,1},{4,6},{5,7},{6,4},{7,5},{8,10},{9,11},{10,... | collective-permute-start | bytes 49160 | tf_op jit(solution)/shard_map/ppermute | solution.py:376
  167.9 27.9 %collective-permute-start.24 = (bf16[64,128]{1,0:T(8,128)(2,1)}, bf16[64,128]{1,0:T(8,128)(2,1)S(1)}, u32[]{:S(2)}, u32[]{:S(2)}) collective-permute-start(bf16[64,128]{1,0:T(8,128)(2,1)} %get-tuple-element.46), channel_id=1, source_target_pairs={{0,3},{1,0},{2,1},{3,2},{4,7},{5,4},{6,5},{7,6},{8,11},{9,8},{10,9... | collective-permute-start | bytes 49160 | tf_op jit(solution)/shard_map/ppermute | solution.py:376
  198.9 21.6 %collective-permute-start.29 = (bf16[32,2048]{1,0:T(8,128)(2,1)S(1)}, bf16[32,2048]{1,0:T(8,128)(2,1)S(1)}, u32[]{:S(2)}, u32[]{:S(2)}) collective-permute-start(bf16[32,2048]{1,0:T(8,128)(2,1)S(1)} %get-tuple-element.54), channel_id=1, source_target_pairs={{0,2},{1,3},{2,0},{3,1},{4,6},{5,7},{6,4},{7,5},{8,10},{9,11},{10,... | collective-permute-start | bytes 393224 | tf_op jit(solution)/shard_map/ppermute | solution.py:389
  213.0 20.8 %collective-permute-start.8 = (bf16[64,2048]{1,0:T(8,128)(2,1)S(1)}, bf16[64,2048]{1,0:T(8,128)(2,1)S(1)}, u32[]{:S(2)}, u32[]{:S(2)}) collective-permute-start(bf16[64,2048]{1,0:T(8,128)(2,1)S(1)} %copy-done.44), channel_id=1, source_target_pairs={{0,1},{1,2},{2,3},{3,0},{4,5},{5,6},{6,7},{7,4},{8,9},{9,10},{10,1... | collective-permute-start | bytes 786440 | tf_op jit(solution)/shard_map/ppermute | solution.py:383
  216.6 17.9 %collective-permute-start.19 = (bf16[64,2048]{1,0:T(8,128)(2,1)S(1)}, bf16[64,2048]{1,0:T(8,128)(2,1)S(1)}, u32[]{:S(2)}, u32[]{:S(2)}) collective-permute-start(bf16[64,2048]{1,0:T(8,128)(2,1)S(1)} %copy-done.45), channel_id=1, source_target_pairs={{0,1},{1,2},{2,3},{3,0},{4,5},{5,6},{6,7},{7,4},{8,9},{9,10},{10,1... | collective-permute-start | bytes 786440 | tf_op jit(solution)/shard_map/ppermute | solution.py:383
  216.7 14.5 %collective-permute-start.28 = (bf16[32,2048]{1,0:T(8,128)(2,1)S(1)}, bf16[32,2048]{1,0:T(8,128)(2,1)S(1)}, u32[]{:S(2)}, u32[]{:S(2)}) collective-permute-start(bf16[32,2048]{1,0:T(8,128)(2,1)S(1)} %get-tuple-element.54), channel_id=1, source_target_pairs={{0,1},{1,2},{2,3},{3,0},{4,5},{5,6},{6,7},{7,4},{8,9},{9,10},{10,1... | collective-permute-start | bytes 393224 | tf_op jit(solution)/shard_map/ppermute | solution.py:389
  217.2 15.2 %collective-permute-start.30 = (bf16[32,2048]{1,0:T(8,128)(2,1)S(1)}, bf16[32,2048]{1,0:T(8,128)(2,1)S(1)}, u32[]{:S(2)}, u32[]{:S(2)}) collective-permute-start(bf16[32,2048]{1,0:T(8,128)(2,1)S(1)} %get-tuple-element.54), channel_id=1, source_target_pairs={{0,3},{1,0},{2,1},{3,2},{4,7},{5,4},{6,5},{7,6},{8,11},{9,8},{10,9... | collective-permute-start | bytes 393224 | tf_op jit(solution)/shard_map/ppermute | solution.py:389
  234.6 15.9 %collective-permute-start.20 = (bf16[64,2048]{1,0:T(8,128)(2,1)S(1)}, bf16[64,2048]{1,0:T(8,128)(2,1)S(1)}, u32[]{:S(2)}, u32[]{:S(2)}) collective-permute-start(bf16[64,2048]{1,0:T(8,128)(2,1)S(1)} %add_convert_fusion.4), channel_id=1, source_target_pairs={{0,1},{1,2},{2,3},{3,0},{4,5},{5,6},{6,7},{7,4},{8,9},{9,10},{10,1... | collective-permute-start | bytes 786440 | tf_op jit(solution)/shard_map/ppermute | solution.py:383
  (56 other events, 687.2 us)
where the time goes:
time: 263 us; the launch traced here: 262 us
  waiting for transfers between devices  112 us (43%)
  Pallas kernels  83.5 us (32%)
  starting transfers between devices  31.1 us (12%)
  other arithmetic  18.7 us (7%)
  local copies, waits for them, and re-layouts  13 us (5%)
    pallas_call x2, Pallas kernels, input_partial(): pl.pallas_call(functools.partial(input_kernel, (n_dp, n_t, g, own_t, rc,...  38.7 us
    ppermute x2, waiting for transfers between devices, per_device(): own = lax.ppermute(own, 'tensor', y_next)  37.6 us
    ppermute x6, waiting for transfers between devices, per_device(): piece = lax.ppermute(piece, 'dp', z_next)  28.7 us
    ppermute x6, waiting for transfers between devices, per_device(): message = lax.ppermute(message, 'dp', z_next)  25.1 us
    pallas_call x2, Pallas kernels, hidden_partial(): pl.pallas_call(functools.partial(hidden_kernel, (n_dp, n_t, g, own_t, rc,...  24.9 us
    pallas_call x2, Pallas kernels, outer(): pl.pallas_call(functools.partial(outer_kernel, owners, count), out_shape=...  13.6 us
    ppermute x3, waiting for transfers between devices, per_device(): lax.ppermute(in_part, 'dp', ring(n_dp, r))  11.9 us
    ppermute x6, starting transfers between devices, per_device(): lax.ppermute(queries[r], 'dp', ring(n_dp, r))  8.88 us
  transfers between devices with their start and end apart: 33, of which 17 were waited for; matrix products, arithmetic and copies ran while one was open for 9% of the time, Pallas kernels for 31%

commit v1 on v0

v1 whole, which is shorter than its diff:
```python
import functools

import jax
import jax.numpy as jnp
from jax import lax
from jax.experimental import pallas as pl
from jax.experimental.pallas import tpu as pltpu
from jax.sharding import PartitionSpec as P

R = 16
TENANTS = 4
BLOCK = 128
SHARES = (1, 2, 1)
LANES = 128
VMEM_LIMIT = 56 * 1024 * 1024

ADAPTER_SCALE = 2.0

NT = (((1,), (1,)), ((), ()))
NN = (((1,), (0,)), ((), ()))


def fdot(lhs, rhs, dims):
    return lax.dot_general(lhs, rhs, dims, preferred_element_type=jnp.float32)


def tile_of(width, most):
    tile = most
    while width % tile:
        tile -= LANES
    return tile


def whole(shape):
    return pl.BlockSpec(shape, lambda *_: (0,) * len(shape))


def tenant_of(meta, owner, own_t):
    return meta[2 + (owner * own_t) // BLOCK]


def hidden_kernel(sizes, meta, *refs):
    n_dp, n_t, g, own_t, rc, tile = sizes
    ny = n_t // 2
    pieces, (w_ref, bd_ref, ad_ref, keep_ref, send_ref, x_scr, xt_scr, p_scr) = refs[:n_dp], refs[n_dp:]
    step = pl.program_id(0)
    z, t = meta[0], meta[1]
    y, c = t // 2, t % 2
    width = w_ref.shape[1]
    hidden_width = keep_ref.shape[2] - LANES

    @pl.when(step == 0)
    def _():
        for k in range(n_dp):
            for j in range(g):
                owner = lax.rem(z + (n_dp - k), n_dp) * g + j
                away = jnp.where(owner % 2 == c, 0, ny)
                x_scr[away + lax.rem(owner // 2 + ny - y, ny)] = pieces[k][j]
        x_all = x_scr[...].reshape(n_t * rc, width)
        xt_scr[...] = x_all.T
        proj = fdot(x_all, bd_ref[...], NT)
        lane = lax.broadcasted_iota(jnp.int32, (rc, TENANTS * R), 1) // R
        zeros = jnp.zeros((rc, LANES - TENANTS * R), jnp.bfloat16)
        for s in range(n_t):
            owner = lax.rem(y + s % ny, ny) * 2 + (c if s < ny else 1 - c)
            own = jnp.where(lane == tenant_of(meta, owner, own_t), proj[s * rc : (s + 1) * rc], 0.0)
            p_scr[s * rc : (s + 1) * rc, :] = (ADAPTER_SCALE * own).astype(jnp.bfloat16)
            out = keep_ref if s < ny else send_ref
            out[s % ny, :, hidden_width:] = jnp.concatenate([own.astype(jnp.bfloat16), zeros], axis=1)

    acc = fdot(w_ref[...], xt_scr[...], NN).T + fdot(p_scr[...], ad_ref[...], NN)
    acc = acc.astype(jnp.bfloat16).reshape(n_t, rc, tile)
    at = pl.ds(pl.multiple_of(step * tile, LANES), tile)
    keep_ref[:, :, at] = acc[:ny]
    send_ref[:, :, at] = acc[ny:]


def hidden_partial(meta, pieces, down_weight, b_down, a_down, n_t, own_t):
    n_dp = len(pieces)
    g, rc, width = pieces[0].shape
    ny = n_t // 2
    hidden_width = down_weight.shape[0]
    tile = tile_of(hidden_width, 512)
    low = TENANTS * R
    out = jax.ShapeDtypeStruct((ny, rc, hidden_width + LANES), jnp.bfloat16)
    return pl.pallas_call(
        functools.partial(hidden_kernel, (n_dp, n_t, g, own_t, rc, tile)),
        out_shape=(out, out),
        grid_spec=pltpu.PrefetchScalarGridSpec(
            num_scalar_prefetch=1,
            grid=(hidden_width // tile,),
            in_specs=[whole((g, rc, width))] * n_dp
            + [
                pl.BlockSpec((tile, width), lambda f, *_: (f, 0)),
                whole((low, width)),
                pl.BlockSpec((low, tile), lambda f, *_: (0, f)),
            ],
            out_specs=[whole(out.shape)] * 2,
            scratch_shapes=[
                pltpu.VMEM((n_t, rc, width), jnp.bfloat16),
                pltpu.VMEM((width, n_t * rc), jnp.bfloat16),
                pltpu.VMEM((n_t * rc, low), jnp.bfloat16),
            ],
        ),
        compiler_params=pltpu.CompilerParams(vmem_limit_bytes=VMEM_LIMIT),
        cost_estimate=pl.CostEstimate(
            flops=2 * n_t * rc * width * hidden_width,
            bytes_accessed=2 * width * hidden_width,
            transcendentals=0,
        ),
        name="hidden_partial",
    )(meta, *pieces, down_weight, b_down, a_down)


def act_kernel(keep_ref, pair_ref, far_ref, dgate_ref, dup_ref, out_ref, low_ref):
    width = out_ref.shape[2]
    total = keep_ref[0].astype(jnp.float32) + pair_ref[0].astype(jnp.float32)
    total = total + far_ref[...].astype(jnp.float32)
    low_ref[...] = total[:, width:].astype(jnp.bfloat16)
    hidden_grad = total[:, :width]
    out_ref[0] = (hidden_grad * dgate_ref[...]).astype(jnp.bfloat16)
    out_ref[1] = (hidden_grad * dup_ref[...]).astype(jnp.bfloat16)


def act(keep, pair, far, dgate, dup):
    ny, rc, padded = keep.shape
    width = padded - LANES
    return pl.pallas_call(
        act_kernel,
        out_shape=(
            jax.ShapeDtypeStruct((2, rc, width), jnp.bfloat16),
            jax.ShapeDtypeStruct((rc, LANES), jnp.bfloat16),
        ),
        grid=(1,),
        in_specs=[
            whole((1, rc, padded)),
            whole((1, rc, padded)),
            whole((rc, padded)),
            whole((rc, width)),
            whole((rc, width)),
        ],
        out_specs=[whole((2, rc, width)), whole((rc, LANES))],
        compiler_params=pltpu.CompilerParams(vmem_limit_bytes=VMEM_LIMIT),
        cost_estimate=pl.CostEstimate(
            flops=4 * rc * width, bytes_accessed=18 * rc * width, transcendentals=0
        ),
        name="act_grads",
    )(keep, pair, far, dgate, dup)


def owner_of(p, y, c, ny):
    return lax.rem(y + ny - p // 2, ny) * 2 + (c if p % 2 == 0 else 1 - c)


def input_kernel(sizes, meta, *refs):
    n_dp, n_t, g, own_t, rc, tile = sizes
    ny = n_t // 2
    pieces, (gw_ref, uw_ref, b_ref, a_ref), refs = refs[:n_t], refs[n_t : n_t + 4], refs[n_t + 4 :]
    outs, (g_scr, u_scr, acc, query) = refs[:n_dp], refs[n_dp:]
    step = pl.program_id(0)
    z, t = meta[0], meta[1]
    y, c = t // 2, t % 2
    rows = n_t * rc
    width = gw_ref.shape[0]

    @pl.when(step == 0)
    def _():
        acc[...] = jnp.zeros_like(acc)
        query[...] = jnp.zeros_like(query)

    for p in range(n_t):
        owner = owner_of(p, y, c, ny)
        slot = lax.rem(owner // g + n_dp - z, n_dp) * g + owner % g
        g_scr[slot] = pieces[p][0]
        u_scr[slot] = pieces[p][1]
    gate = g_scr[...].reshape(rows, tile).T
    up = u_scr[...].reshape(rows, tile).T
    low = lax.broadcasted_iota(jnp.int32, (2 * R * TENANTS, rows), 0) % (2 * R)
    query[...] += jnp.where(low < R, fdot(b_ref[...], gate, NN), fdot(b_ref[...], up, NN))
    acc[...] += fdot(gw_ref[...], gate, NN) + fdot(uw_ref[...], up, NN)

    @pl.when(step == pl.num_programs(0) - 1)
    def _():
        lane = lax.broadcasted_iota(jnp.int32, (rc, 2 * R * TENANTS), 1) // (2 * R)
        turned = query[...].T
        own = []
        for r in range(n_dp):
            for j in range(g):
                s = r * g + j
                tenant = tenant_of(meta, lax.rem(z + r, n_dp) * g + j, own_t)
                own.append(jnp.where(lane == tenant, turned[s * rc : (s + 1) * rc], 0.0))
        own = (ADAPTER_SCALE * jnp.concatenate(own, axis=0)).astype(jnp.bfloat16)
        cols = tile_of(width, 512)
        for d in range(0, width, cols):
            part = acc[d : d + cols, :].T + fdot(own, a_ref[:, d : d + cols], NN)
            part = part.astype(jnp.bfloat16)
            for r in range(n_dp):
                outs[r][:, d : d + cols] = part[r * g * rc : (r + 1) * g * rc]


def input_partial(meta, pieces, gate_weight, up_weight, b_gu, a_gu, n_dp, own_t):
    n_t = len(pieces)
    _, rc, hidden_width = pieces[0].shape
    g = n_t // n_dp
    width = gate_weight.shape[0]
    tile = tile_of(hidden_width, 512)
    low = 2 * R * TENANTS
    rows = n_t * rc
    outs = [jax.ShapeDtypeStruct((g * rc, width), jnp.bfloat16)] * n_dp
    return pl.pallas_call(
        functools.partial(input_kernel, (n_dp, n_t, g, own_t, rc, tile)),
        out_shape=outs,
        grid_spec=pltpu.PrefetchScalarGridSpec(
            num_scalar_prefetch=1,
            grid=(hidden_width // tile,),
            in_specs=[pl.BlockSpec((2, rc, tile), lambda f, *_: (0, 0, f))] * n_t
            + [
                pl.BlockSpec((width, tile), lambda f, *_: (0, f)),
                pl.BlockSpec((width, tile), lambda f, *_: (0, f)),
                pl.BlockSpec((low, tile), lambda f, *_: (0, f)),
                whole((low, width)),
            ],
            out_specs=[whole(o.shape) for o in outs],
            scratch_shapes=[
                pltpu.VMEM((n_t, rc, tile), jnp.bfloat16),
                pltpu.VMEM((n_t, rc, tile), jnp.bfloat16),
                pltpu.VMEM((width, rows), jnp.float32),
                pltpu.VMEM((low, rows), jnp.float32),
            ],
        ),
        compiler_params=pltpu.CompilerParams(vmem_limit_bytes=VMEM_LIMIT),
        cost_estimate=pl.CostEstimate(
            flops=4 * rows * width * hidden_width,
            bytes_accessed=4 * width * hidden_width,
            transcendentals=0,
        ),
        name="input_partial",
    )(meta, *pieces, gate_weight, up_weight, b_gu, a_gu)


def query_kernel(own_t, count, meta, *refs):
    pieces, b_ref, out_ref = refs[:count], refs[count], refs[count + 1]
    gate = jnp.concatenate([piece[0] for piece in pieces], axis=0)
    up = jnp.concatenate([piece[1] for piece in pieces], axis=0)
    lane = lax.broadcasted_iota(jnp.int32, out_ref.shape, 1)
    query = jnp.where(lane % (2 * R) < R, fdot(gate, b_ref[...], NT), fdot(up, b_ref[...], NT))
    tenant = tenant_of(meta, meta[1], own_t)
    out_ref[...] = jnp.where(lane // (2 * R) == tenant, query, 0.0).astype(jnp.bfloat16)


def own_query(meta, pieces, b_gu, own_t):
    out = jax.ShapeDtypeStruct((own_t, b_gu.shape[0]), jnp.bfloat16)
    return pl.pallas_call(
        functools.partial(query_kernel, own_t, len(pieces)),
        out_shape=out,
        grid_spec=pltpu.PrefetchScalarGridSpec(
            num_scalar_prefetch=1,
            grid=(1,),
            in_specs=[whole(piece.shape) for piece in pieces] + [whole(b_gu.shape)],
            out_specs=whole(out.shape),
        ),
        compiler_params=pltpu.CompilerParams(vmem_limit_bytes=VMEM_LIMIT),
        name="own_query",
    )(meta, *pieces, b_gu)


def outer_kernel(plan, layers, counts, meta, *refs):
    sources, j_of, owner_at = plan
    pieces, left_ref, out_ref = refs[: counts], refs[counts], refs[counts + 1]
    owners = [owner_at(s, meta) for s in range(len(sources))]
    for layer in range(layers):
        left = jnp.concatenate([left_ref[layer, owner] for owner in owners], axis=1)
        right = [pieces[k][j_of(s, layer)] for s, ks in enumerate(sources) for k in ks]
        out_ref[layer] = ADAPTER_SCALE * fdot(left, jnp.concatenate(right, axis=0), NN)


def outer(meta, pieces, left, plan, layers, name):
    width = pieces[0].shape[2]
    tile = tile_of(width, 512)
    rows = left.shape[2]
    return pl.pallas_call(
        functools.partial(outer_kernel, plan, layers, len(pieces)),
        out_shape=jax.ShapeDtypeStruct((layers, rows, width), jnp.float32),
        grid_spec=pltpu.PrefetchScalarGridSpec(
            num_scalar_prefetch=1,
            grid=(width // tile,),
            in_specs=[
                pl.BlockSpec(piece.shape[:2] + (tile,), lambda f, *_: (0, 0, f)) for piece in pieces
            ]
            + [whole(left.shape)],
            out_specs=pl.BlockSpec((layers, rows, tile), lambda f, *_: (0, 0, f)),
        ),
        compiler_params=pltpu.CompilerParams(vmem_limit_bytes=VMEM_LIMIT),
        name=name,
    )(meta, *pieces, left)


def spread_kernel(tenant_at, rows, meta, *refs):
    parts, out_ref = refs[:-1], refs[-1]
    out_ref[...] = jnp.zeros_like(out_ref)
    at = 0
    for part in parts:
        for k in range(part.shape[0] // rows):
            tenant = tenant_at(at, meta)
            term = part[k * rows : (k + 1) * rows].astype(jnp.float32)
            out_ref[tenant] = out_ref[tenant] + ADAPTER_SCALE * term
            at += 1


def spread(meta, parts, tenant_at, rows, name):
    width = parts[0].shape[1]
    out = jax.ShapeDtypeStruct((TENANTS, rows, width), jnp.float32)
    tile = tile_of(width, 1024)
    return pl.pallas_call(
        functools.partial(spread_kernel, tenant_at, rows),
        out_shape=out,
        grid_spec=pltpu.PrefetchScalarGridSpec(
            num_scalar_prefetch=1,
            grid=(width // tile,),
            in_specs=[pl.BlockSpec((part.shape[0], tile), lambda f, *_: (0, f)) for part in parts],
            out_specs=pl.BlockSpec((TENANTS, rows, tile), lambda f, *_: (0, 0, f)),
        ),
        compiler_params=pltpu.CompilerParams(vmem_limit_bytes=VMEM_LIMIT),
        name=name,
    )(meta, *parts)


def ring(n, by):
    return [(k, (k + by) % n) for k in range(n)]


def add32(*terms):
    return sum(term.astype(jnp.float32) for term in terms)


def after(value, *done):
    return lax.optimization_barrier((value,) + done)[0]


def per_device(
    layer_input,
    out_grad,
    gate_pre,
    up_pre,
    adapter_acts,
    gate_weight,
    up_weight,
    down_weight,
    adapter_a_gu,
    adapter_b_gu,
    adapter_a_down,
    adapter_b_down,
    block_tenant,
):
    n_dp, n_t = lax.axis_size("dp"), lax.axis_size("tensor")
    ny = n_t // 2
    z, t = lax.axis_index("dp"), lax.axis_index("tensor")
    own_rows, width = out_grad.shape
    own_t, hidden_width = gate_pre.shape
    tokens = adapter_acts.shape[0]
    g = own_rows // own_t
    assert own_rows == BLOCK and g * own_t == own_rows and n_t == 2 * ny and n_t == g * n_dp
    chunks, at = [], 0
    for share in SHARES:
        chunks.append((at, own_t * share // sum(SHARES)))
        at += chunks[-1][1]

    meta = jnp.concatenate([jnp.stack([z, t]).astype(jnp.int32), block_tenant])
    b_down = adapter_b_down.reshape(TENANTS * R, width)
    a_down = jnp.transpose(adapter_a_down, (0, 2, 1)).reshape(TENANTS * R, hidden_width)
    b_gu = adapter_b_gu.reshape(TENANTS * 2 * R, hidden_width)
    a_gu = jnp.transpose(adapter_a_gu, (0, 2, 1)).reshape(TENANTS * 2 * R, width)

    pair = [(k, k ^ 1) for k in range(n_t)]
    y_next = ring(n_t, 2)
    z_next = ring(n_dp, 1)

    grads, last = [], None
    for at, rc in chunks:
        piece = out_grad.reshape(g, own_t, width)[:, at : at + rc]
        if last is not None:
            piece = after(piece, last)
        pieces = [piece]
        for _ in range(n_dp - 1):
            piece = lax.ppermute(piece, "dp", z_next)
            pieces.append(piece)
        last = pieces[n_dp - 2]
        grads.append(pieces)

    hidden, dgates, dups = [], [], []
    for at, rc in chunks:
        gate_value = gate_pre[at : at + rc].astype(jnp.float32)
        up_value = up_pre[at : at + rc].astype(jnp.float32)
        sigmoid_value = jax.nn.sigmoid(gate_value)
        hidden.append((gate_value * sigmoid_value * up_value).astype(jnp.bfloat16))
        dgates.append(up_value * sigmoid_value * (1.0 + gate_value * (1.0 - sigmoid_value)))
        dups.append(gate_value * sigmoid_value)
    hidden = jnp.concatenate(hidden, axis=0)
    onehot = (
        jnp.arange(TENANTS, dtype=jnp.int32)[:, None] == jnp.repeat(block_tenant, BLOCK)[None, :]
    ).astype(jnp.bfloat16)
    acts = adapter_acts.T.reshape(3, 1, R, tokens) * onehot[None, :, None, :]
    acts = acts.reshape(3, TENANTS * R, n_t, own_t).transpose(0, 2, 1, 3)

    def first(q, done):
        pieces = [after(grads[q][0], *done)] + grads[q][1:]
        keep, send = hidden_partial(meta, pieces, down_weight, b_down, a_down, n_t, own_t)
        return keep, lax.ppermute(send, "tensor", pair)

    def reduce(keep, other):
        message = add32(keep[ny - 1], other[ny - 1]).astype(jnp.bfloat16)
        for s in range(ny - 1):
            far = lax.ppermute(message, "tensor", y_next)
            if s < ny - 2:
                message = add32(keep[ny - 2 - s], other[ny - 2 - s], far).astype(jnp.bfloat16)
        return message, far

    def gather(own, done):
        own = after(own, *done)
        pieces = [own, lax.ppermute(own, "tensor", pair)]
        for _ in range(ny - 1):
            own = lax.ppermute(own, "tensor", y_next)
            pieces += [own, lax.ppermute(own, "tensor", pair)]
        return pieces

    def second(pieces, done):
        pieces = [after(pieces[0], *done)] + pieces[1:]
        outs = input_partial(meta, pieces, gate_weight, up_weight, b_gu, a_gu, n_dp, own_t)
        there = [lax.ppermute(outs[r], "dp", ring(n_dp, r)) for r in range(1, n_dp)]
        return outs, there

    def finish(outs, there, rc):
        return add32(outs[0], *there).astype(jnp.bfloat16).reshape(g, rc, width)

    keep_a, other_a = first(0, ())
    sum_a, far_a = reduce(keep_a, other_a)
    own_a, low_a = act(keep_a, other_a, far_a, dgates[0], dups[0])
    full_a = gather(own_a, ())

    keep_b, other_b = first(1, (own_a,))
    sum_b, far_b = reduce(keep_b, other_b)
    keep_c, other_c = first(2, (sum_b,))
    sum_c, far_c = reduce(keep_c, other_c)
    own_b, low_b = act(after(keep_b, sum_c), other_b, far_b, dgates[1], dups[1])
    full_b = gather(own_b, ())
    own_c, low_c = act(after(keep_c, own_b), other_c, far_c, dgates[2], dups[2])

    query = own_query(meta, [own_a, own_b, own_c], b_gu, own_t)
    query_there = [lax.ppermute(query, "dp", ring(n_dp, r)) for r in range(1, n_dp)]

    outs_a, there_a = second(full_a, (query,))

    low = jnp.concatenate([low_a, low_b, low_c], axis=0)[:, : TENANTS * R]
    a_part = fdot(after(low, outs_a[0]), hidden, (((0,), (0,)), ((), ())))
    a_part = a_part.reshape(TENANTS, R, hidden_width).sum(0).astype(jnp.bfloat16)
    a_column = [a_part] + [lax.ppermute(a_part, "tensor", ring(n_t, 2 * s)) for s in range(1, ny)]

    query = add32(after(query, a_part), *query_there).astype(jnp.bfloat16)
    queries = [query] + [lax.ppermute(query, "tensor", ring(n_t, 2 * s)) for s in range(1, ny)]
    queries = jnp.stack(queries)
    queries = [queries, lax.ppermute(queries, "tensor", pair)]

    full_c = gather(own_c, (full_b[2],))
    outs_b, there_b = second(full_b, (queries[0], full_c[0]))

    a_beside = lax.ppermute(jnp.concatenate(a_column, axis=0), "tensor", pair)
    rows_query = []
    for j in range(g):
        owner = z * g + j
        from_far = lax.rem(t // 2 + ny - owner // 2, ny)
        mine = jnp.where(owner % 2 == t % 2, queries[0], queries[1])
        rows_query.append(lax.dynamic_index_in_dim(mine, from_far, 0, keepdims=False))
    rows_query = jnp.concatenate(rows_query, axis=0)
    in_part = fdot(after(rows_query, outs_b[0]), layer_input, (((0,), (0,)), ((), ())))
    in_part = in_part.reshape(TENANTS, 2 * R, width).sum(0).astype(jnp.bfloat16)
    in_all = [in_part] + [lax.ppermute(in_part, "dp", ring(n_dp, r)) for r in range(1, n_dp)]

    outs_c, there_c = second(full_c, (in_part,))

    def gathered_plan():
        sources = [[q * n_t + p for q in range(len(chunks))] for p in range(n_t)]
        return sources, lambda s, layer: layer, lambda s, m: owner_of(s, m[1] // 2, m[1] % 2, ny)

    def grads_plan():
        sources = [[q * n_dp + s // g for q in range(len(chunks))] for s in range(n_t)]
        return (
            sources,
            lambda s, layer: s % g,
            lambda s, m: lax.rem(m[0] + (n_dp - s // g), n_dp) * g + s % g,
        )

    x_pieces = [x for pieces in grads for x in pieces]
    grad_b_down = outer(meta, x_pieces, after(acts[2:], outs_c[0]), grads_plan(), 1, "down_outer")
    gu_pieces = full_a + full_b + full_c
    left = after(acts[:2], grad_b_down)
    grad_b_gu = outer(meta, gu_pieces, left, gathered_plan(), 2, "gate_up_outer")
    grad_b_down = grad_b_down.reshape(TENANTS, R, width)
    grad_b_gu = grad_b_gu.reshape(2, TENANTS, R, hidden_width).transpose(1, 0, 2, 3)
    grad_b_gu = grad_b_gu.reshape(TENANTS, 2 * R, hidden_width)

    def column_tenant(p, m):
        owner = lax.rem(m[1] // 2 + ny - p % ny, ny) * 2
        return tenant_of(m, owner + (m[1] % 2 if p < ny else 1 - m[1] % 2), own_t)

    grad_a_down = spread(meta, a_column + [a_beside], column_tenant, R, "spread_a_down")
    grad_a_gu = spread(
        meta, in_all, lambda r, m: m[2 + lax.rem(m[0] + n_dp - r, n_dp)], 2 * R, "spread_a_gu"
    )

    parts = [
        finish(outs, there, rc)
        for (outs, there), (_, rc) in zip(
            ((outs_a, there_a), (outs_b, there_b), (outs_c, there_c)), chunks
        )
    ]
    block_input_grad = jnp.concatenate(parts, axis=1).reshape(own_rows, width)
    return (
        block_input_grad,
        grad_a_gu.transpose(0, 2, 1),
        grad_b_gu,
        grad_a_down.transpose(0, 2, 1),
        grad_b_down,
    )


def solution(mesh):
    placed = (
        P(("groups", "dp"), "tensor"),
        P(("groups", "dp"), "tensor"),
        P(("groups", "tensor"), "dp"),
        P(("groups", "tensor"), "dp"),
        P("groups", None),
        P("tensor", "dp"),
        P("tensor", "dp"),
        P("dp", "tensor"),
        P(None, "tensor", None),
        P(None, None, "dp"),
        P(None, "dp", None),
        P(None, None, "tensor"),
        P("groups"),
    )
    return jax.shard_map(
        per_device,
        mesh=mesh,
        in_specs=placed,
        out_specs=(
            P(("groups", "dp"), "tensor"),
            P("groups", "tensor", None),
            P("groups", None, "dp"),
            P("groups", "dp", None),
            P("groups", None, "tensor"),
        ),
        check_vma=False,
    )
```

time: 263 us -> 274 us (1.042)
  Pallas kernels: 83.5 us -> 123 us
  waiting for transfers between devices: 112 us -> 84.9 us
  starting transfers between devices: 31.1 us -> 35 us
  other arithmetic: 18.7 us -> 15 us
    ppermute x23 -> x30, waiting for transfers between devices: 69.7 us -> 39.1 us  [the longest x9 17.5 us: second(): there = [lax.ppermute(outs[r], 'dp', ring(n_dp, r)) for r in range(1, n_dp)]]
    ppermute x6 -> x9, waiting for transfers between devices: 28.7 us -> 45.8 us  [per_device(): piece = lax.ppermute(piece, 'dp', z_next)]
    pallas_call x2 -> x3, Pallas kernels: 38.7 us -> 54.9 us  [input_partial(): pl.pallas_call(functools.partial(input_kernel, (n_dp, n_t, g, own_t, rc,...]
    pallas_call x2 -> x3, Pallas kernels: 24.9 us -> 36.8 us  [hidden_partial(): pl.pallas_call(functools.partial(hidden_kernel, (n_dp, n_t, g, own_t, rc,...]
    ppermute x3, waiting for transfers between devices: 11.9 us -> 0.01 us  [per_device(): lax.ppermute(in_part, 'dp', ring(n_dp, r))]
    pallas_call x2 -> x5, Pallas kernels: 13.6 us -> 23.1 us  [the longest x2 12.8 us: outer(): pl.pallas_call(functools.partial(outer_kernel, plan, layers, len(pieces))...]
    mul x8 -> x0, other arithmetic: 6.15 us -> none  [the longest x1 2.72 us: per_device(): dup = gate_value * sigmoid_value]
    ppermute x23 -> x30, starting transfers between devices: 19.6 us -> 25 us  [the longest x9 12.6 us: second(): there = [lax.ppermute(outs[r], 'dp', ring(n_dp, r)) for r in range(1, n_dp)]]
  transfers between devices with their start and end apart: 33 -> 43, of which waited for: 17 -> 12; matrix products, arithmetic and copies ran while one was open for 9% -> 8% of each run, Pallas kernels for 31% -> 40%
where the time goes in v1:
time: 274 us; the launch traced here: 273 us
  Pallas kernels  123 us (45%)
  waiting for transfers between devices  84.9 us (31%)
  starting transfers between devices  35 us (13%)
  other arithmetic  15 us (5%)
  local copies, waits for them, and re-layouts  12.4 us (5%)
    pallas_call x3, Pallas kernels, input_partial(): pl.pallas_call(functools.partial(input_kernel, (n_dp, n_t, g, own_t, rc,...  54.9 us
    ppermute x9, waiting for transfers between devices, per_device(): piece = lax.ppermute(piece, 'dp', z_next)  45.8 us
    pallas_call x3, Pallas kernels, hidden_partial(): pl.pallas_call(functools.partial(hidden_kernel, (n_dp, n_t, g, own_t, rc,...  36.8 us
    ppermute x9, waiting for transfers between devices, second(): there = [lax.ppermute(outs[r], 'dp', ring(n_dp, r)) for r in range(1, n_dp)]  17.5 us
    ppermute x3, waiting for transfers between devices, reduce(): far = lax.ppermute(message, 'tensor', y_next)  14.3 us
    pallas_call x2, Pallas kernels, outer(): pl.pallas_call(functools.partial(outer_kernel, plan, layers, len(pieces))...  12.8 us
    ppermute x9, starting transfers between devices, second(): there = [lax.ppermute(outs[r], 'dp', ring(n_dp, r)) for r in range(1, n_dp)]  12.6 us
    pallas_call x3, Pallas kernels, act(): pl.pallas_call(act_kernel, out_shape=(jax.ShapeDtypeStruct((2, rc, width)...  7.78 us
  transfers between devices with their start and end apart: 43, of which 12 were waited for; matrix products, arithmetic and copies ran while one was open for 8% of the time, Pallas kernels for 40%

profile of v1, /device:TPU:0, one launch (start us, length us, event | category | flops | bytes accessed | tf_op | source)
XLA Modules:
  0.0 272.7 jit_solution(17829746281289965926)
XLA Ops:
  1.7 3.1 %collective-permute-start = (bf16[1,32,2048]{2,1,0:T(8,128)(2,1)S(1)}, bf16[1,32,2048]{2,1,0:T(8,128)(2,1)S(1)}, u32[]{:S(2)}, u32[]{:S(2)}) collective-permute-start(bf16[1,32,2048]{2,1,0:T(8,128)(2,1)S(1)} %get-tuple-element.92.refs_0_), channel_id=1, source_target_pairs={{0,1},{1,2},{2,3},{3,0},{4,5},{5,6},{6,7},{7,4},{8,9},{9,10},{10,1... | collective-permute-start | bytes 393224 | tf_op jit(solution)/shard_map/ppermute | solution.py:385
  4.8 5.5 %collective-permute-done.refs_1_ = bf16[1,32,2048]{2,1,0:T(8,128)(2,1)S(1)} collective-permute-done((bf16[1,32,2048]{2,1,0:T(8,128)(2,1)S(1)}, bf16[1,32,2048]{2,1,0:T(8,128)(2,1)S(1)}, u32[]{:S(2)}, u32[]{:S(2)}) %collective-permute-start) | collective-permute-done | bytes 131104 | tf_op jit(solution)/shard_map/ppermute | solution.py:385
  10.3 6.8 %collective-permute-done.1.refs_2_ = bf16[1,32,2048]{2,1,0:T(8,128)(2,1)S(1)} collective-permute-done((bf16[1,32,2048]{2,1,0:T(8,128)(2,1)S(1)}, bf16[1,32,2048]{2,1,0:T(8,128)(2,1)S(1)}, u32[]{:S(2)}, u32[]{:S(2)}) %collective-permute-start.1) | collective-permute-done | bytes 131104 | tf_op jit(solution)/shard_map/ppermute | solution.py:385
  19.5 5.7 %collective-permute-done.2.refs_3_ = bf16[1,32,2048]{2,1,0:T(8,128)(2,1)S(1)} collective-permute-done((bf16[1,32,2048]{2,1,0:T(8,128)(2,1)S(1)}, bf16[1,32,2048]{2,1,0:T(8,128)(2,1)S(1)}, u32[]{:S(2)}, u32[]{:S(2)}) %collective-permute-start.2) | collective-permute-done | bytes 131104 | tf_op jit(solution)/shard_map/ppermute | solution.py:385
  25.8 12.1 %hidden_partial.3 = (bf16[2,32,3712]{2,1,0:T(8,128)(2,1)}, bf16[2,32,3712]{2,1,0:T(8,128)(2,1)}) custom-call(s32[6]{0:T(128)} %pad_add_fusion.meta, bf16[1,32,2048]{2,1,0:T(8,128)(2,1)} %copy-done.9, bf16[1,32,2048]{2,1,0:T(8,128)(2,1)} %copy-done.20, bf16[1,32,2048]{2,1,0:T(8,128)(2,1)} %copy-done.21, bf16[1,32,2048]{2,1,0:T(8,128)(2,1)} %copy-done.22, ...), custom_call_target="tpu_custom_call" | custom-call | flops 1879048192 | bytes 14680064 | tf_op jit(solution)/shard_map/hidden_partial/pallas_call | solution.py:86
  38.0 10.4 %collective-permute-done.6.refs_2_.refs_6_ = bf16[1,64,2048]{2,1,0:T(8,128)(2,1)S(1)} collective-permute-done((bf16[1,64,2048]{2,1,0:T(8,128)(2,1)S(1)}, bf16[1,64,2048]{2,1,0:T(8,128)(2,1)S(1)}, u32[]{:S(2)}, u32[]{:S(2)}) %collective-permute-start.6) | collective-permute-done | bytes 262176 | tf_op jit(solution)/shard_map/ppermute | solution.py:385
  53.0 4.1 %collective-permute-done.4.far_ref = bf16[32,3712]{1,0:T(8,128)(2,1)S(1)} collective-permute-done((bf16[32,3712]{1,0:T(8,128)(2,1)S(1)}, bf16[32,3712]{1,0:T(8,128)(2,1)S(1)}, u32[]{:S(2)}, u32[]{:S(2)}) %collective-permute-start.4) | collective-permute-done | bytes 237600 | tf_op jit(solution)/shard_map/ppermute | solution.py:413
  60.9 12.8 %hidden_partial.4 = (bf16[2,64,3712]{2,1,0:T(8,128)(2,1)}, bf16[2,64,3712]{2,1,0:T(8,128)(2,1)}) custom-call(s32[6]{0:T(128)} %pad_add_fusion.meta, bf16[1,64,2048]{2,1,0:T(8,128)(2,1)} %copy-done.5, bf16[1,64,2048]{2,1,0:T(8,128)(2,1)} %copy-done.14, bf16[1,64,2048]{2,1,0:T(8,128)(2,1)} %copy-done.15, bf16[1,64,2048]{2,1,0:T(8,128)(2,1)} %copy-done.16, ...), custom_call_target="tpu_custom_call" | custom-call | flops 3758096384 | bytes 14680064 | tf_op jit(solution)/shard_map/hidden_partial/pallas_call | solution.py:86
  73.7 7.6 %collective-permute-done.9.refs_1_.refs_9_ = bf16[1,32,2048]{2,1,0:T(8,128)(2,1)S(1)} collective-permute-done((bf16[1,32,2048]{2,1,0:T(8,128)(2,1)S(1)}, bf16[1,32,2048]{2,1,0:T(8,128)(2,1)S(1)}, u32[]{:S(2)}, u32[]{:S(2)}) %collective-permute-start.9) | collective-permute-done | bytes 131104 | tf_op jit(solution)/shard_map/ppermute | solution.py:385
  81.4 6.9 %collective-permute-done.10.refs_2_.refs_10_ = bf16[1,32,2048]{2,1,0:T(8,128)(2,1)S(1)} collective-permute-done((bf16[1,32,2048]{2,1,0:T(8,128)(2,1)S(1)}, bf16[1,32,2048]{2,1,0:T(8,128)(2,1)S(1)}, u32[]{:S(2)}, u32[]{:S(2)}) %collective-permute-start.10) | collective-permute-done | bytes 131104 | tf_op jit(solution)/shard_map/ppermute | solution.py:385
  92.1 2.9 %collective-permute-done.11.refs_3_.refs_11_ = bf16[1,32,2048]{2,1,0:T(8,128)(2,1)S(1)} collective-permute-done((bf16[1,32,2048]{2,1,0:T(8,128)(2,1)S(1)}, bf16[1,32,2048]{2,1,0:T(8,128)(2,1)S(1)}, u32[]{:S(2)}, u32[]{:S(2)}) %collective-permute-start.11) | collective-permute-done | bytes 131104 | tf_op jit(solution)/shard_map/ppermute | solution.py:385
  95.7 11.9 %hidden_partial.5 = (bf16[2,32,3712]{2,1,0:T(8,128)(2,1)}, bf16[2,32,3712]{2,1,0:T(8,128)(2,1)}) custom-call(s32[6]{0:T(128)} %pad_add_fusion.meta, bf16[1,32,2048]{2,1,0:T(8,128)(2,1)} %copy-done.10, bf16[1,32,2048]{2,1,0:T(8,128)(2,1)} %copy-done.23, bf16[1,32,2048]{2,1,0:T(8,128)(2,1)} %copy-done.24, bf16[1,32,2048]{2,1,0:T(8,128)(2,1)} %copy-done.25, ...), custom_call_target="tpu_custom_call" | custom-call | flops 1879048192 | bytes 14680064 | tf_op jit(solution)/shard_map/hidden_partial/pallas_call | solution.py:86
  113.7 10.2 %collective-permute-done.13.far_ref = bf16[64,3712]{1,0:T(8,128)(2,1)S(1)} collective-permute-done((bf16[64,3712]{1,0:T(8,128)(2,1)}, bf16[64,3712]{1,0:T(8,128)(2,1)S(1)}, u32[]{:S(2)}, u32[]{:S(2)}) %collective-permute-start.13) | collective-permute-done | bytes 475168 | tf_op jit(solution)/shard_map/ppermute | solution.py:413
  124.7 3.1 %act_grads.4 = (bf16[2,64,3584]{2,1,0:T(8,128)(2,1)}, bf16[64,128]{1,0:T(8,128)(2,1)}) custom-call(bf16[2,64,3712]{2,1,0:T(8,128)(2,1)} %get-tuple-element.55.keep_ref, bf16[2,64,3712]{2,1,0:T(8,128)(2,1)} %copy-done.6, bf16[64,3712]{1,0:T(8,128)(2,1)} %copy-done.27, f32[64,3584]{1,0:T(8,128)} %get-tuple-element.88.dgate_ref, ...), custom_call_target="tpu_custom_call" | custom-call | flops 917504 | bytes 4128768 | tf_op jit(solution)/shard_map/act_grads/pallas_call | solution.py:128
  131.8 3.8 %own_query.1 = bf16[128,128]{1,0:T(8,128)(2,1)} custom-call(s32[6]{0:T(128)} %pad_add_fusion.meta, bf16[2,32,3584]{2,1,0:T(8,128)(2,1)} %get-tuple-element.59.refs_0_, bf16[2,64,3584]{2,1,0:T(8,128)(2,1)} %get-tuple-element.70.refs_1_.refs_0_.refs_4_, bf16[2,32,3584]{2,1,0:T(8,128)(2,1)} %get-tuple-element.76.refs_2_.refs_0_.refs_8_, bf16[128,3584]{1,0:T(8,128)(2,1)} %bitcast.50), custom_call_target="tpu_custom_call" | custom-call | tf_op jit(solution)/shard_map/own_query/pallas_call | solution.py:253
  137.7 17.9 %input_partial.3 = (bf16[32,2048]{1,0:T(8,128)(2,1)}, bf16[32,2048]{1,0:T(8,128)(2,1)}, bf16[32,2048]{1,0:T(8,128)(2,1)}, bf16[32,2048]{1,0:T(8,128)(2,1)}) custom-call(s32[6]{0:T(128)} %pad_add_fusion.meta, bf16[2,32,3584]{2,1,0:T(8,128)(2,1)} %get-tuple-element.59.refs_0_, bf16[2,32,3584]{2,1,0:T(8,128)(2,1)} %collective-permute-done.15.refs_1_, ...), custom_call_target="tpu_custom_call" | custom-call | flops 3758096384 | bytes 29360128 | tf_op jit(solution)/shard_map/input_partial/pallas_call | solution.py:210
  172.1 7.3 %collective-permute-done.33.refs_2_.refs_10_ = bf16[2,32,3584]{2,1,0:T(8,128)(2,1)S(1)} collective-permute-done((bf16[2,32,3584]{2,1,0:T(8,128)(2,1)S(1)}, bf16[2,32,3584]{2,1,0:T(8,128)(2,1)S(1)}, u32[]{:S(2)}, u32[]{:S(2)}) %collective-permute-start.33) | collective-permute-done | bytes 458784 | tf_op jit(solution)/shard_map/ppermute | solution.py:422
  180.0 19.3 %input_partial.4 = (bf16[64,2048]{1,0:T(8,128)(2,1)}, bf16[64,2048]{1,0:T(8,128)(2,1)}, bf16[64,2048]{1,0:T(8,128)(2,1)}, bf16[64,2048]{1,0:T(8,128)(2,1)}) custom-call(s32[6]{0:T(128)} %pad_add_fusion.meta, bf16[2,64,3584]{2,1,0:T(8,128)(2,1)} %get-tuple-element.70.refs_1_.refs_0_.refs_4_, bf16[2,64,3584]{2,1,0:T(8,128)(2,1)} %copy-done.4, ...), custom_call_target="tpu_custom_call" | custom-call | flops 7516192768 | bytes 29360128 | tf_op jit(solution)/shard_map/input_partial/pallas_call | solution.py:210
  201.9 17.7 %input_partial.5 = (bf16[32,2048]{1,0:T(8,128)(2,1)}, bf16[32,2048]{1,0:T(8,128)(2,1)}, bf16[32,2048]{1,0:T(8,128)(2,1)}, bf16[32,2048]{1,0:T(8,128)(2,1)}) custom-call(s32[6]{0:T(128)} %pad_add_fusion.meta, bf16[2,32,3584]{2,1,0:T(8,128)(2,1)} %get-tuple-element.76.refs_2_.refs_0_.refs_8_, bf16[2,32,3584]{2,1,0:T(8,128)(2,1)} %collective-permute-done.32.refs_1_.refs_9_, ...), custom_call_target="tpu_custom_call" | custom-call | flops 3758096384 | bytes 29360128 | tf_op jit(solution)/shard_map/input_partial/pallas_call | solution.py:210
  227.1 3.9 %spread_a_down.1 = f32[4,16,3584]{2,1,0:T(8,128)} custom-call(s32[6]{0:T(128)} %pad_add_fusion.meta, bf16[16,3584]{1,0:T(8,128)(2,1)} %copy-done.17, bf16[16,3584]{1,0:T(8,128)(2,1)} %copy-done.28, bf16[32,3584]{1,0:T(8,128)(2,1)} %copy-done.34), custom_call_target="tpu_custom_call" | custom-call | tf_op jit(solution)/shard_map/spread_a_down/pallas_call | solution.py:314
  231.0 4.7 %down_outer.1 = f32[1,64,2048]{2,1,0:T(8,128)} custom-call(s32[6]{0:T(128)} %pad_add_fusion.meta, bf16[1,32,2048]{2,1,0:T(8,128)(2,1)} %copy-done.9, bf16[1,32,2048]{2,1,0:T(8,128)(2,1)} %copy-done.20, bf16[1,32,2048]{2,1,0:T(8,128)(2,1)} %copy-done.21, bf16[1,32,2048]{2,1,0:T(8,128)(2,1)} %copy-done.22, bf16[1,64,2048]{2,1,0:T(8,128)(2,1)} %copy-done.5, ...), custom_call_target="tpu_custom_call" | custom-call | tf_op jit(solution)/shard_map/down_outer/pallas_call | solution.py:281
  235.7 8.1 %gate_up_outer.1 = f32[2,64,3584]{2,1,0:T(8,128)} custom-call(s32[6]{0:T(128)} %pad_add_fusion.meta, bf16[2,32,3584]{2,1,0:T(8,128)(2,1)} %get-tuple-element.59.refs_0_, bf16[2,32,3584]{2,1,0:T(8,128)(2,1)} %collective-permute-done.15.refs_1_, bf16[2,32,3584]{2,1,0:T(8,128)(2,1)} %copy-done.7, bf16[2,32,3584]{2,1,0:T(8,128)(2,1)} %collective-permute-done.17.refs_3_, ...), custom_call_target="tpu_custom_call" | custom-call | tf_op jit(solution)/shard_map/gate_up_outer/pallas_call | solution.py:281
  243.8 2.9 %copy.21 = f32[4,2,16,3584]{3,2,1,0:T(8,128)} copy(f32[4,2,16,3584]{3,2,0,1:T(8,128)} %bitcast.54) | data formatting | bytes 3670016 | tf_op jit(solution)/shard_map/transpose | solution.py:498
  255.7 16.0 %collective-permute-done.29 = bf16[64,2048]{1,0:T(8,128)(2,1)S(1)} collective-permute-done((bf16[64,2048]{1,0:T(8,128)(2,1)S(1)}, bf16[64,2048]{1,0:T(8,128)(2,1)S(1)}, u32[]{:S(2)}, u32[]{:S(2)}) %collective-permute-start.29) | collective-permute-done | bytes 262176 | tf_op jit(solution)/shard_map/ppermute | solution.py:429
  (212 shorter events, 66.9 us)
Async XLA Ops:
  19.5 18.4 %collective-permute-start.5 = (bf16[1,64,2048]{2,1,0:T(8,128)(2,1)S(1)}, bf16[1,64,2048]{2,1,0:T(8,128)(2,1)S(1)}, u32[]{:S(2)}, u32[]{:S(2)}) collective-permute-start(bf16[1,64,2048]{2,1,0:T(8,128)(2,1)S(1)} %slice.74.refs_0_.refs_4_), channel_id=1, source_target_pairs={{0,1},{1,2},{2,3},{3,0},{4,5},{5,6},{6,7},{7,4},{8,9},{9,10},{10,1... | collective-permute-start | bytes 786440 | tf_op jit(solution)/shard_map/ppermute | solution.py:385
  88.2 21.7 %collective-permute-start.16 = (bf16[2,32,3584]{2,1,0:T(8,128)(2,1)S(1)}, bf16[2,32,3584]{2,1,0:T(8,128)(2,1)S(1)}, u32[]{:S(2)}, u32[]{:S(2)}) collective-permute-start(bf16[2,32,3584]{2,1,0:T(8,128)(2,1)S(1)} %copy-done.1), channel_id=1, source_target_pairs={{0,8},{4,12},{8,0},{12,4},{1,9},{5,13},{9,1},{13,5},{2,10},{6,14},... | collective-permute-start | bytes 1376264 | tf_op jit(solution)/shard_map/ppermute | solution.py:422
  109.4 26.2 %collective-permute-start.15 = (bf16[2,32,3584]{2,1,0:T(8,128)(2,1)S(1)}, bf16[2,32,3584]{2,1,0:T(8,128)(2,1)}, u32[]{:S(2)}, u32[]{:S(2)}) collective-permute-start(bf16[2,32,3584]{2,1,0:T(8,128)(2,1)S(1)} %copy-done.1), channel_id=1, source_target_pairs={{0,4},{4,0},{8,12},{12,8},{1,5},{5,1},{9,13},{13,9},{2,6},{6,2},{1... | collective-permute-start | bytes 1376264 | tf_op jit(solution)/shard_map/ppermute | solution.py:420
  109.9 25.8 %collective-permute-start.17 = (bf16[2,32,3584]{2,1,0:T(8,128)(2,1)S(1)}, bf16[2,32,3584]{2,1,0:T(8,128)(2,1)}, u32[]{:S(2)}, u32[]{:S(2)}) collective-permute-start(bf16[2,32,3584]{2,1,0:T(8,128)(2,1)S(1)} %collective-permute-done.16.refs_2_), channel_id=1, source_target_pairs={{0,4},{4,0},{8,12},{12,8},{1,5},{5,1},{9,13},{13,9},{2,6},{6,2},{1... | collective-permute-start | bytes 1376264 | tf_op jit(solution)/shard_map/ppermute | solution.py:423
  127.8 32.6 %collective-permute-start.25 = (bf16[2,64,3584]{2,1,0:T(8,128)(2,1)}, bf16[2,64,3584]{2,1,0:T(8,128)(2,1)S(1)}, u32[]{:S(2)}, u32[]{:S(2)}) collective-permute-start(bf16[2,64,3584]{2,1,0:T(8,128)(2,1)} %get-tuple-element.70.refs_1_.refs_0_.refs_4_), channel_id=1, source_target_pairs={{0,8},{4,12},{8,0},{12,4},{1,9},{5,13},{9,1},{13,5},{2,10},{6,14},... | collective-permute-start | bytes 2752520 | tf_op jit(solution)/shard_map/ppermute | solution.py:422
  129.4 42.4 %collective-permute-start.26 = (bf16[2,64,3584]{2,1,0:T(8,128)(2,1)}, bf16[2,64,3584]{2,1,0:T(8,128)(2,1)S(1)}, u32[]{:S(2)}, u32[]{:S(2)}) collective-permute-start(bf16[2,64,3584]{2,1,0:T(8,128)(2,1)} %get-tuple-element.70.refs_1_.refs_0_.refs_4_), channel_id=1, source_target_pairs={{0,4},{4,0},{8,12},{12,8},{1,5},{5,1},{9,13},{13,9},{2,6},{6,2},{1... | collective-permute-start | bytes 2752520 | tf_op jit(solution)/shard_map/ppermute | solution.py:420
  135.5 22.6 %collective-permute-start.23 = (bf16[128,128]{1,0:T(8,128)(2,1)}, bf16[128,128]{1,0:T(8,128)(2,1)S(1)}, u32[]{:S(2)}, u32[]{:S(2)}) collective-permute-start(bf16[128,128]{1,0:T(8,128)(2,1)} %own_query.1), channel_id=1, source_target_pairs={{0,3},{1,0},{2,1},{3,2},{4,7},{5,4},{6,5},{7,6},{8,11},{9,8},{10,9... | collective-permute-start | bytes 98312 | tf_op jit(solution)/shard_map/ppermute | solution.py:449
  135.7 22.5 %collective-permute-start.22 = (bf16[128,128]{1,0:T(8,128)(2,1)}, bf16[128,128]{1,0:T(8,128)(2,1)}, u32[]{:S(2)}, u32[]{:S(2)}) collective-permute-start(bf16[128,128]{1,0:T(8,128)(2,1)} %own_query.1), channel_id=1, source_target_pairs={{0,2},{1,3},{2,0},{3,1},{4,6},{5,7},{6,4},{7,5},{8,10},{9,11},{10,... | collective-permute-start | bytes 98312 | tf_op jit(solution)/shard_map/ppermute | solution.py:449
  135.8 23.0 %collective-permute-start.21 = (bf16[128,128]{1,0:T(8,128)(2,1)}, bf16[128,128]{1,0:T(8,128)(2,1)}, u32[]{:S(2)}, u32[]{:S(2)}) collective-permute-start(bf16[128,128]{1,0:T(8,128)(2,1)} %own_query.1), channel_id=1, source_target_pairs={{0,1},{1,2},{2,3},{3,0},{4,5},{5,6},{6,7},{7,4},{8,9},{9,10},{10,1... | collective-permute-start | bytes 98312 | tf_op jit(solution)/shard_map/ppermute | solution.py:449
  160.4 19.0 %collective-permute-start.27 = (bf16[2,64,3584]{2,1,0:T(8,128)(2,1)S(1)}, bf16[2,64,3584]{2,1,0:T(8,128)(2,1)}, u32[]{:S(2)}, u32[]{:S(2)}) collective-permute-start(bf16[2,64,3584]{2,1,0:T(8,128)(2,1)S(1)} %collective-permute-done.25.refs_2_.refs_6_), channel_id=1, source_target_pairs={{0,4},{4,0},{8,12},{12,8},{1,5},{5,1},{9,13},{13,9},{2,6},{6,2},{1... | collective-permute-start | bytes 2752520 | tf_op jit(solution)/shard_map/ppermute | solution.py:423
  164.0 55.6 %collective-permute-start.20 = (bf16[32,2048]{1,0:T(8,128)(2,1)}, bf16[32,2048]{1,0:T(8,128)(2,1)}, u32[]{:S(2)}, u32[]{:S(2)}) collective-permute-start(bf16[32,2048]{1,0:T(8,128)(2,1)} %get-tuple-element.63), channel_id=1, source_target_pairs={{0,3},{1,0},{2,1},{3,2},{4,7},{5,4},{6,5},{7,6},{8,11},{9,8},{10,9... | collective-permute-start | bytes 393224 | tf_op jit(solution)/shard_map/ppermute | solution.py:429
  168.9 51.7 %collective-permute-start.19 = (bf16[32,2048]{1,0:T(8,128)(2,1)}, bf16[32,2048]{1,0:T(8,128)(2,1)}, u32[]{:S(2)}, u32[]{:S(2)}) collective-permute-start(bf16[32,2048]{1,0:T(8,128)(2,1)} %get-tuple-element.62), channel_id=1, source_target_pairs={{0,2},{1,3},{2,0},{3,1},{4,6},{5,7},{6,4},{7,5},{8,10},{9,11},{10,... | collective-permute-start | bytes 393224 | tf_op jit(solution)/shard_map/ppermute | solution.py:429
  171.8 51.7 %collective-permute-start.18 = (bf16[32,2048]{1,0:T(8,128)(2,1)}, bf16[32,2048]{1,0:T(8,128)(2,1)}, u32[]{:S(2)}, u32[]{:S(2)}) collective-permute-start(bf16[32,2048]{1,0:T(8,128)(2,1)} %get-tuple-element.61), channel_id=1, source_target_pairs={{0,1},{1,2},{2,3},{3,0},{4,5},{5,6},{6,7},{7,4},{8,9},{9,10},{10,1... | collective-permute-start | bytes 393224 | tf_op jit(solution)/shard_map/ppermute | solution.py:429
  179.4 20.3 %collective-permute-start.32 = (bf16[2,32,3584]{2,1,0:T(8,128)(2,1)S(1)}, bf16[2,32,3584]{2,1,0:T(8,128)(2,1)}, u32[]{:S(2)}, u32[]{:S(2)}) collective-permute-start(bf16[2,32,3584]{2,1,0:T(8,128)(2,1)S(1)} %copy-done.2), channel_id=1, source_target_pairs={{0,4},{4,0},{8,12},{12,8},{1,5},{5,1},{9,13},{13,9},{2,6},{6,2},{1... | collective-permute-start | bytes 1376264 | tf_op jit(solution)/shard_map/ppermute | solution.py:420
  179.4 20.8 %collective-permute-start.34 = (bf16[2,32,3584]{2,1,0:T(8,128)(2,1)S(1)}, bf16[2,32,3584]{2,1,0:T(8,128)(2,1)}, u32[]{:S(2)}, u32[]{:S(2)}) collective-permute-start(bf16[2,32,3584]{2,1,0:T(8,128)(2,1)S(1)} %collective-permute-done.33.refs_2_.refs_10_), channel_id=1, source_target_pairs={{0,4},{4,0},{8,12},{12,8},{1,5},{5,1},{9,13},{13,9},{2,6},{6,2},{1... | collective-permute-start | bytes 1376264 | tf_op jit(solution)/shard_map/ppermute | solution.py:423
  200.2 23.9 %collective-permute-start.42 = (bf16[32,3584]{1,0:T(8,128)(2,1)S(1)}, bf16[32,3584]{1,0:T(8,128)(2,1)S(1)}, u32[]{:S(2)}, u32[]{:S(2)}) collective-permute-start(bf16[32,3584]{1,0:T(8,128)(2,1)S(1)} %copy-done.35), channel_id=1, source_target_pairs={{0,4},{4,0},{8,12},{12,8},{1,5},{5,1},{9,13},{13,9},{2,6},{6,2},{1... | collective-permute-start | bytes 688136 | tf_op jit(solution)/shard_map/ppermute | solution.py:466
  200.3 23.9 %collective-permute-start.38 = (bf16[32,2048]{1,0:T(8,128)(2,1)S(1)}, bf16[32,2048]{1,0:T(8,128)(2,1)S(1)}, u32[]{:S(2)}, u32[]{:S(2)}) collective-permute-start(bf16[32,2048]{1,0:T(8,128)(2,1)S(1)} %reduce_sum.19.refs_0_), channel_id=1, source_target_pairs={{0,1},{1,2},{2,3},{3,0},{4,5},{5,6},{6,7},{7,4},{8,9},{9,10},{10,1... | collective-permute-start | bytes 393224 | tf_op jit(solution)/shard_map/ppermute | solution.py:476
  219.6 27.1 %collective-permute-start.39 = (bf16[32,2048]{1,0:T(8,128)(2,1)S(1)}, bf16[32,2048]{1,0:T(8,128)(2,1)S(1)}, u32[]{:S(2)}, u32[]{:S(2)}) collective-permute-start(bf16[32,2048]{1,0:T(8,128)(2,1)S(1)} %reduce_sum.19.refs_0_), channel_id=1, source_target_pairs={{0,2},{1,3},{2,0},{3,1},{4,6},{5,7},{6,4},{7,5},{8,10},{9,11},{10,... | collective-permute-start | bytes 393224 | tf_op jit(solution)/shard_map/ppermute | solution.py:476
  220.7 28.2 %collective-permute-start.40 = (bf16[32,2048]{1,0:T(8,128)(2,1)S(1)}, bf16[32,2048]{1,0:T(8,128)(2,1)S(1)}, u32[]{:S(2)}, u32[]{:S(2)}) collective-permute-start(bf16[32,2048]{1,0:T(8,128)(2,1)S(1)} %reduce_sum.19.refs_0_), channel_id=1, source_target_pairs={{0,3},{1,0},{2,1},{3,2},{4,7},{5,4},{6,5},{7,6},{8,11},{9,8},{10,9... | collective-permute-start | bytes 393224 | tf_op jit(solution)/shard_map/ppermute | solution.py:476
  223.5 29.2 %collective-permute-start.37 = (bf16[32,2048]{1,0:T(8,128)(2,1)}, bf16[32,2048]{1,0:T(8,128)(2,1)S(1)}, u32[]{:S(2)}, u32[]{:S(2)}) collective-permute-start(bf16[32,2048]{1,0:T(8,128)(2,1)} %get-tuple-element.80), channel_id=1, source_target_pairs={{0,3},{1,0},{2,1},{3,2},{4,7},{5,4},{6,5},{7,6},{8,11},{9,8},{10,9... | collective-permute-start | bytes 393224 | tf_op jit(solution)/shard_map/ppermute | solution.py:429
  224.1 30.0 %collective-permute-start.36 = (bf16[32,2048]{1,0:T(8,128)(2,1)}, bf16[32,2048]{1,0:T(8,128)(2,1)S(1)}, u32[]{:S(2)}, u32[]{:S(2)}) collective-permute-start(bf16[32,2048]{1,0:T(8,128)(2,1)} %get-tuple-element.79), channel_id=1, source_target_pairs={{0,2},{1,3},{2,0},{3,1},{4,6},{5,7},{6,4},{7,5},{8,10},{9,11},{10,... | collective-permute-start | bytes 393224 | tf_op jit(solution)/shard_map/ppermute | solution.py:429
  224.2 30.0 %collective-permute-start.35 = (bf16[32,2048]{1,0:T(8,128)(2,1)}, bf16[32,2048]{1,0:T(8,128)(2,1)S(1)}, u32[]{:S(2)}, u32[]{:S(2)}) collective-permute-start(bf16[32,2048]{1,0:T(8,128)(2,1)} %get-tuple-element.78), channel_id=1, source_target_pairs={{0,1},{1,2},{2,3},{3,0},{4,5},{5,6},{6,7},{7,4},{8,9},{9,10},{10,1... | collective-permute-start | bytes 393224 | tf_op jit(solution)/shard_map/ppermute | solution.py:429
  248.9 22.8 %collective-permute-start.29 = (bf16[64,2048]{1,0:T(8,128)(2,1)S(1)}, bf16[64,2048]{1,0:T(8,128)(2,1)S(1)}, u32[]{:S(2)}, u32[]{:S(2)}) collective-permute-start(bf16[64,2048]{1,0:T(8,128)(2,1)S(1)} %copy-done.50), channel_id=1, source_target_pairs={{0,2},{1,3},{2,0},{3,1},{4,6},{5,7},{6,4},{7,5},{8,10},{9,11},{10,... | collective-permute-start | bytes 786440 | tf_op jit(solution)/shard_map/ppermute | solution.py:429
  252.7 19.1 %collective-permute-start.28 = (bf16[64,2048]{1,0:T(8,128)(2,1)S(1)}, bf16[64,2048]{1,0:T(8,128)(2,1)S(1)}, u32[]{:S(2)}, u32[]{:S(2)}) collective-permute-start(bf16[64,2048]{1,0:T(8,128)(2,1)S(1)} %copy-done.49), channel_id=1, source_target_pairs={{0,1},{1,2},{2,3},{3,0},{4,5},{5,6},{6,7},{7,4},{8,9},{9,10},{10,1... | collective-permute-start | bytes 786440 | tf_op jit(solution)/shard_map/ppermute | solution.py:429
  (71 other events, 1023.9 us)
